TPU v7x, 32 devices: a whole 2x2x4 slice. The times are simulated.
32 devices in a mesh: dp: 8 (over z, x), ctx: 4 (over y, core).
Axes of the slice: x: 2, y: 2, z: 4, core: 2. Of those that a mesh axis runs over, the one named last changes fastest.
Arguments:
- tokens: bfloat16 [16, 1024, 1088], P('dp', 'ctx'), may hold values from -6 to 6
- positions: int32 [16, 1024], P('dp'), may hold values from 0 to 1023, as said below
- w_qkv: bfloat16 [3551232], P(('dp', 'ctx')), may hold values from -0.1875 to 0.1875
- w_out: bfloat16 [1183744], P(('dp', 'ctx')), may hold values from -0.75 to 0.75
- w_up: bfloat16 [4734976], P(('dp', 'ctx')), may hold values from -0.1875 to 0.1875
- w_down: bfloat16 [4734976], P(('dp', 'ctx')), may hold values from -0.09375 to 0.09375
- small_params: bfloat16 [13056], P(('dp', 'ctx')), may hold values from -1.2 to 1.6, as said below
- cotangent: bfloat16 [16, 1024, 1088], P('dp', 'ctx'), may hold values from -6 to 6
Outputs:
- result: bfloat16 [16, 1024, 1088], P('dp', 'ctx')
- grad_tokens: bfloat16 [16, 1024, 1088], P('dp', 'ctx')
- grad_qkv: float32 [3551232], P(('dp', 'ctx'))
- grad_out: float32 [1183744], P(('dp', 'ctx'))
- grad_up: float32 [4734976], P(('dp', 'ctx'))
- grad_down: float32 [4734976], P(('dp', 'ctx'))
- grad_small: float32 [13056], P(('dp', 'ctx'))
Inputs may be any that keep to these rules, and one draw needn't show every extreme that they name: Each row is a permutation of 0 to 1023. Spans are runs of 128 positions; slot block c (slots c * 2 * 128 onward) holds, in rising order, span j and then span 2 * 4 - 1 - j, with j differing between blocks and sequences. `small_params`: gains near one and biases of either sign, in the layout of the argument.
All inputs are finite; a program needn't handle non-finite values.
Results may differ from a plain program's by a relative error of at most 0.013.
Values may be sent and summed in bfloat16 or wider, within the bound.
No kernel may reach another device: no remote copies, remote signals or barrier semaphores. Data moves between devices by JAX's collectives and lax.ppermute only.
A program may use at most 256 MiB of HBM per device.

v0:
```python
import jax
import jax.numpy as jnp
from jax import lax
from jax.experimental import pallas as pl
from jax.experimental.pallas import tpu as pltpu
from jax.sharding import Mesh, PartitionSpec as P

HEADS = 17
HEAD_DIM = 64
FF = 4352
LANES = 8
WIDE = 1152
SWAP = ((0, 1), (1, 0))
OWNERS = ("dp", "y")


def layer_stats(values):
    center = values - jnp.mean(values, axis=-1, keepdims=True)
    inverse = lax.rsqrt(jnp.mean(center * center, axis=-1, keepdims=True) + 1e-05)
    return (center * inverse, inverse)


def norm_back(upstream, normed, inverse, gain_vector):
    scaled = upstream * gain_vector
    return inverse * (
        scaled
        - jnp.mean(scaled, axis=-1, keepdims=True)
        - normed * jnp.mean(scaled * normed, axis=-1, keepdims=True)
    )


def lead_dot(left_side, right_side):
    return lax.dot_general(
        left_side, right_side, (((0,), (0,)), ((), ())), preferred_element_type=jnp.float32
    )


def tail_dot(left_side, right_side):
    return lax.dot_general(
        left_side, right_side, (((1,), (1,)), ((), ())), preferred_element_type=jnp.float32
    )


def gate_and_slope(values):
    rate = (2.0 / jnp.pi) ** 0.5
    square = values * values
    bend = jnp.tanh(rate * values * (1.0 + 0.044715 * square))
    share = 0.5 * (1.0 + bend)
    slope = share + 0.5 * values * (1.0 - bend * bend) * rate * (1.0 + 0.134145 * square)
    return values * share, slope


def pack_small(values, width):
    room = LANES * width - values.shape[-1]
    padded = jnp.pad(values, [(0, 0)] * (values.ndim - 1) + [(0, room)])
    return padded.reshape(values.shape[:-1] + (LANES, width))


def gather_packed(block, core):
    own = lax.all_gather(block, OWNERS, axis=0, tiled=True)
    other = lax.ppermute(own, "core", SWAP)
    even = jnp.where(core == 0, own, other)
    odd = jnp.where(core == 0, other, own)
    shape = (-1, 1, LANES, block.shape[1])
    return jnp.concatenate([even.reshape(shape), odd.reshape(shape)], axis=1)


def scatter_packed(packed, core):
    even, odd = packed[:, 0], packed[:, 1]
    keep = jnp.where(core == 0, even, odd)
    give = jnp.where(core == 0, odd, even)
    got = lax.ppermute(give, "core", SWAP)
    pair = (keep.astype(jnp.float32) + got.astype(jnp.float32)).astype(jnp.bfloat16)
    return lax.psum_scatter(pair, OWNERS, scatter_dimension=0, tiled=True)[0]


def dot_rows(left, right):
    return lax.dot_general(
        left, right, (((1,), (0,)), ((), ())), preferred_element_type=jnp.float32
    )


def bias_of(key_places, query_places):
    return jnp.where(key_places <= query_places, 0.0, -1e30).astype(jnp.float32)


def per_pair(one_pair):
    pair = 2 * HEAD_DIM
    full = HEADS // 2

    def step(number, carry):
        one_pair(pl.multiple_of(number * pair, pair), 2 * number, 2)
        return carry

    lax.fori_loop(0, full, step, 0)
    if HEADS % 2:
        one_pair(full * pair, 2 * full, 1)


def lanes_at(start, block):
    return pl.ds(block * WIDE + start, 2 * HEAD_DIM)


def stand(parts):
    if len(parts) == 1:
        parts = parts + [jnp.zeros_like(parts[0])]
    return jnp.concatenate(parts, axis=0).T


def only_head(values, number, heads):
    if heads == 1:
        return values
    lane = lax.broadcasted_iota(jnp.int32, values.shape, 1)
    inside = lane < HEAD_DIM if number == 0 else lane >= HEAD_DIM
    return jnp.where(inside, values, jnp.zeros_like(values))


def join_heads(parts):
    if len(parts) == 1:
        return parts[0]
    lane = lax.broadcasted_iota(jnp.int32, parts[0].shape, 1)
    return jnp.where(lane < HEAD_DIM, parts[0], parts[1])


def attend_kernel(
    own_ref, other_ref, query_ref, key_ref, mixed_ref, log_ref, low_bias, up_bias
):
    half = own_ref.shape[0] // 2
    low_bias[...] = bias_of(key_ref[: 2 * half], query_ref[:, :half])
    up_bias[...] = bias_of(key_ref[2 * half :], query_ref[:, half:])

    def one_pair(start, first, heads):
        q = own_ref[:, lanes_at(start, 0)] * jnp.asarray(HEAD_DIM**-0.5, jnp.bfloat16)
        k_own, v_own = own_ref[:, lanes_at(start, 1)], own_ref[:, lanes_at(start, 2)]
        k_other, v_other = other_ref[:, lanes_at(start, 0)], other_ref[:, lanes_at(start, 1)]
        k_low = jnp.concatenate([k_own[:half], k_other[:half]], axis=0)
        k_up = jnp.concatenate([k_own[half:], k_other[half:]], axis=0)
        v_low = jnp.concatenate([v_own[:half], v_other[:half]], axis=0).T
        v_up = jnp.concatenate([v_own[half:], v_other[half:]], axis=0).T
        low_parts, up_parts = [], []
        for number in range(heads):
            rows = slice(number * HEAD_DIM, (number + 1) * HEAD_DIM)
            q_head = only_head(q, number, heads)
            s = tail_dot(k_low, q_head[:half]) + low_bias[...]
            top = jnp.max(s, axis=0, keepdims=True)
            e = jnp.exp(s - top)
            total = jnp.sum(e, axis=0, keepdims=True)
            mixed = dot_rows(v_low[rows], e.astype(jnp.bfloat16)) / total
            low_parts.append(mixed)
            log_ref[pl.ds(first + number, 1), :half] = top + jnp.log(total)
            s_low = tail_dot(k_low, q_head[half:])
            s_up = tail_dot(k_up, q_head[half:]) + up_bias[...]
            top = jnp.maximum(
                jnp.max(s_low, axis=0, keepdims=True), jnp.max(s_up, axis=0, keepdims=True)
            )
            e_low = jnp.exp(s_low - top)
            e_up = jnp.exp(s_up - top)
            total = jnp.sum(e_low, axis=0, keepdims=True) + jnp.sum(e_up, axis=0, keepdims=True)
            mixed = dot_rows(v_low[rows], e_low.astype(jnp.bfloat16))
            mixed = mixed + dot_rows(v_up[rows], e_up.astype(jnp.bfloat16))
            up_parts.append(mixed / total)
            log_ref[pl.ds(first + number, 1), half:] = top + jnp.log(total)
        mixed_ref[:half, lanes_at(start, 0)] = stand(low_parts).astype(jnp.bfloat16)
        mixed_ref[half:, lanes_at(start, 0)] = stand(up_parts).astype(jnp.bfloat16)

    per_pair(one_pair)


def attend_back_kernel(
    own_ref,
    other_ref,
    query_ref,
    key_ref,
    mixed_ref,
    log_ref,
    grad_ref,
    own_out,
    other_out,
    low_bias,
    up_bias,
):
    half = own_ref.shape[0] // 2
    factor = HEAD_DIM**-0.5
    low_bias[...] = bias_of(key_ref[: 2 * half], query_ref[:, :half])
    up_bias[...] = bias_of(key_ref[2 * half :], query_ref[:, half:])

    def one_pair(start, first, heads):
        lanes = lanes_at(start, 0)
        q = own_ref[:, lanes] * jnp.asarray(factor, jnp.bfloat16)
        grad = grad_ref[:, lanes]
        product = (grad.astype(jnp.float32) * mixed_ref[:, lanes].astype(jnp.float32)).T
        q_heads = [only_head(q, number, heads) for number in range(heads)]
        grad_heads = [only_head(grad, number, heads) for number in range(heads)]
        deltas = [
            jnp.sum(product[number * HEAD_DIM : (number + 1) * HEAD_DIM], axis=0, keepdims=True)
            for number in range(heads)
        ]
        logs = [log_ref[pl.ds(first + number, 1), :] for number in range(heads)]
        dq_low = [None] * heads
        dq_up = [None] * heads
        for source, out, place, block in (
            (own_ref, own_out, 0, 1),
            (other_ref, other_out, 1, 0),
        ):
            klanes, vlanes = lanes_at(start, block), lanes_at(start, block + 1)
            bias_rows = slice(place * half, (place + 1) * half)
            for upper in (False, True):
                rows = slice(half, None) if upper else slice(0, half)
                k = source[rows, klanes]
                v = source[rows, vlanes]
                k_turned = k.T
                dk_parts, dv_parts = [], []
                for number in range(heads):
                    head_rows = slice(number * HEAD_DIM, (number + 1) * HEAD_DIM)
                    first_query = half if upper else 0
                    q_head = q_heads[number][first_query:]
                    grad_head = grad_heads[number][first_query:]
                    s = tail_dot(k, q_head)
                    if upper:
                        s = s + up_bias[bias_rows]
                    else:
                        s = jnp.concatenate([s[:, :half] + low_bias[bias_rows], s[:, half:]], axis=1)
                    p = jnp.exp(s - logs[number][:, first_query:])
                    dp = tail_dot(v, grad_head)
                    ds = (p * (dp - deltas[number][:, first_query:])).astype(jnp.bfloat16)
                    dv_parts.append(dot_rows(p.astype(jnp.bfloat16), grad[first_query:]))
                    dk_parts.append(dot_rows(ds, q[first_query:]))
                    turned = dot_rows(k_turned[head_rows], ds)
                    low = None if upper else turned[:, :half]
                    up = turned if upper else turned[:, half:]
                    if low is not None:
                        dq_low[number] = low if dq_low[number] is None else dq_low[number] + low
                    dq_up[number] = up if dq_up[number] is None else dq_up[number] + up
                out[rows, klanes] = join_heads(dk_parts).astype(jnp.bfloat16)
                out[rows, vlanes] = join_heads(dv_parts).astype(jnp.bfloat16)
        own_out[:half, lanes] = (stand(dq_low) * factor).astype(jnp.bfloat16)
        own_out[half:, lanes] = (stand(dq_up) * factor).astype(jnp.bfloat16)

    per_pair(one_pair)


def add_kernel(own_ref, got_ref, out_ref):
    total = own_ref[...].astype(jnp.float32) + got_ref[...].astype(jnp.float32)
    out_ref[...] = total.astype(out_ref.dtype)


def add_received(own, got):
    rows = own.shape[0]
    block = (rows, WIDE)
    return pl.pallas_call(
        add_kernel,
        grid=(2,),
        in_specs=[
            pl.BlockSpec(block, lambda i: (0, i + 1)),
            pl.BlockSpec(block, lambda i: (0, i)),
        ],
        out_specs=pl.BlockSpec(block, lambda i: (0, i + 1)),
        out_shape=jax.ShapeDtypeStruct(own.shape, own.dtype),
        input_output_aliases={0: 0},
        compiler_params=pltpu.CompilerParams(vmem_limit_bytes=32 * 1024 * 1024),
        cost_estimate=pl.CostEstimate(flops=1 << 20, bytes_accessed=7 << 20, transcendentals=0),
    )(own, got)


def kernel_call(body, outs, half, cost):
    return pl.pallas_call(
        body,
        out_shape=outs,
        scratch_shapes=[pltpu.VMEM((2 * half, half), jnp.float32)] * 2,
        compiler_params=pltpu.CompilerParams(vmem_limit_bytes=48 * 1024 * 1024),
        cost_estimate=pl.CostEstimate(flops=cost, bytes_accessed=12 << 20, transcendentals=cost // 256),
    )


def outer_kernel(left_ref, right_ref, out_ref):
    out_ref[...] = lead_dot(left_ref[...], right_ref[...]).astype(out_ref.dtype)


def outer(left, right):
    rows, count = left.shape
    width = right.shape[1]
    step = 256
    return pl.pallas_call(
        outer_kernel,
        grid=(count // step,),
        in_specs=[
            pl.BlockSpec((rows, step), lambda i: (0, i)),
            pl.BlockSpec((rows, width), lambda i: (0, 0)),
        ],
        out_specs=pl.BlockSpec((step, width), lambda i: (i, 0)),
        out_shape=jax.ShapeDtypeStruct((count, width), jnp.bfloat16),
        compiler_params=pltpu.CompilerParams(vmem_limit_bytes=32 * 1024 * 1024),
        cost_estimate=pl.CostEstimate(
            flops=2 * rows * count * width, bytes_accessed=16 << 20, transcendentals=0
        ),
    )(left, right)


def attend(own, other, query_places, key_places):
    rows = own.shape[0]
    outs = (
        jax.ShapeDtypeStruct((rows, WIDE), jnp.bfloat16),
        jax.ShapeDtypeStruct((HEADS, rows), jnp.float32),
    )
    call = kernel_call(attend_kernel, outs, rows // 2, 1 << 30)
    return call(own, other, query_places, key_places)


def attend_back(own, other, query_places, key_places, mixed, logs, grad):
    outs = (
        jax.ShapeDtypeStruct(own.shape, jnp.bfloat16),
        jax.ShapeDtypeStruct(other.shape, jnp.bfloat16),
    )
    call = kernel_call(attend_back_kernel, outs, own.shape[0] // 2, 1 << 30)
    return call(own, other, query_places, key_places, mixed, logs, grad)


ALL = ("dp", "y", "core")


def round_low(values):
    return values.astype(jnp.bfloat16)


def one_hot_columns(targets, width):
    line = lax.broadcasted_iota(jnp.int32, (width, targets.shape[0]), 0)
    return (line == targets[None, :]).astype(jnp.bfloat16)


def swap_with(values, axis, bit):
    count = lax.axis_size(axis)
    return lax.ppermute(values, axis, [(here, here ^ (1 << bit)) for here in range(count)])


def near_owners(order, dp_bits, each):
    owner = (lax.axis_index("dp") * 2 + lax.axis_index("y")) * 2 + lax.axis_index("core")
    bits = dp_bits + 2
    column = jnp.arange(each << bits, dtype=jnp.int32)
    place, inner = column // each, column % each
    far = jnp.zeros_like(place)
    for number, (axis, bit) in enumerate(order):
        weight = {"core": 0, "y": 1, "dp": 2 + bit}[axis]
        far = far + (((place >> (bits - 1 - number)) & 1) << weight)
    return (owner ^ far) * each + inner


def give_first(left, right, order):
    half = left.shape[1] // 2
    return swap_with(round_low(lead_dot(left[:, half:], right)), *order[0])


def keep_first(left, right, got):
    half = left.shape[1] // 2
    kept = round_low(lead_dot(left[:, :half], right))
    return round_low(kept.astype(jnp.float32) + got.astype(jnp.float32))


def double(values, axis, bit):
    return jnp.concatenate([values, swap_with(values, axis, bit)], axis=0)


tie = lax.optimization_barrier


def send_half(values, axis, bit):
    return swap_with(values[values.shape[0] // 2 :], axis, bit)


def add_half(values, got):
    half = values.shape[0] // 2
    return round_low(values[:half].astype(jnp.float32) + got.astype(jnp.float32))


def halve(values, axis, bit):
    return add_half(values, send_half(values, axis, bit))


def spread_blocks(values, width):
    spare = jnp.zeros((values.shape[0], WIDE - width), values.dtype)
    parts = []
    for number in range(3):
        parts += [values[:, number * width : (number + 1) * width], spare]
    return jnp.concatenate(parts, axis=1)


def pick_blocks(values, width):
    return jnp.concatenate(
        [values[:, number * WIDE : number * WIDE + width] for number in range(3)], axis=1
    )


def local(tokens, positions, w_qkv, w_out, w_up, w_down, small_params, cotangent):
    seqs_here, local_len, model_width = tokens.shape
    span = local_len // 2
    rows = seqs_here * local_len
    half = rows // 2
    y = lax.axis_index("y")
    core = lax.axis_index("core")
    groups = lax.axis_size("dp")
    owners = groups * 4
    small_len = small_params.shape[0]
    whole_rows = model_width % owners == 0
    each = model_width // owners
    dp_bits = groups.bit_length() - 1

    def trade(values):
        mine = lax.dynamic_index_in_dim(values, y, 0, keepdims=False)
        give = lax.dynamic_index_in_dim(values, 1 - y, 0, keepdims=False)
        got = lax.ppermute(give, "y", SWAP)
        return jnp.concatenate([mine[:span], got[:span], mine[span:], got[span:]], axis=0)

    def trade_back(values):
        mine = jnp.concatenate([values[:span], values[half : half + span]], axis=0)
        give = jnp.concatenate([values[span:half], values[half + span :]], axis=0)
        got = lax.ppermute(give, "y", SWAP)
        first = jnp.where(y == 0, mine, got)
        second = jnp.where(y == 0, got, mine)
        return jnp.stack([first, second])

    place_row = lax.dynamic_index_in_dim(positions, y, 0, keepdims=False)

    def places_of(core_index):
        near = lax.dynamic_slice_in_dim(place_row, (2 * y + core_index) * local_len, local_len)
        far = lax.dynamic_slice_in_dim(place_row, (2 - 2 * y + core_index) * local_len, local_len)
        return jnp.concatenate([near[:span], far[:span]]), jnp.concatenate([near[span:], far[span:]])

    own_low, own_up = places_of(core)
    other_low, other_up = places_of(1 - core)
    query_places = jnp.concatenate([own_low, own_up])[None, :]
    key_places = jnp.concatenate([own_low, other_low, own_up, other_up])[:, None]

    inputs = trade(tokens)
    grad_rows = trade(cotangent)
    if whole_rows:
        steps = [("dp", bit) for bit in range(dp_bits)]
        order_a = [("core", 0), steps[0], ("y", 0)] + steps[1:]
        order_b = [("core", 0), ("y", 0), steps[0]] + steps[1:]
        near_a = near_owners(order_a, dp_bits, each)
        near_b = near_owners(order_b, dp_bits, each)
        turn_a = one_hot_columns(near_a, model_width)
        turn_b = one_hot_columns(near_b, model_width)
        head_a = one_hot_columns(near_a, WIDE)
        head_b = one_hot_columns(near_b, WIDE)
        room = -(each + 1) % 8
        held = each + 1 + room
        column = jnp.arange(owners * held, dtype=jnp.int32)
        inside = column % held
        spread = jnp.where(inside < each, column // held * each + inside, -1)
        head_spread = one_hot_columns(spread, WIDE)
        spread = one_hot_columns(spread, model_width)
        blocks = jnp.concatenate(
            [
                spread_blocks(w_qkv.reshape(each, 3 * model_width), model_width),
                w_out.reshape(each, model_width),
            ],
            axis=1,
        )
        extra = jnp.pad(
            small_params.reshape(1, -1), [(0, room), (0, blocks.shape[1] - small_len)]
        )
        blocks = jnp.concatenate([blocks, extra], axis=0)
        blocks = lax.all_gather(blocks, ALL, axis=0, tiled=True)
        down_mat = lax.all_gather(w_down.reshape(-1, model_width), ALL, axis=0, tiled=True)
        up_part = w_up.reshape(each, FF)
        for step in order_a[:2:-1]:
            up_part = double(up_part, *step)
        up_cut = FF // 2
        blocks, up_part, inputs, grad_rows, query_places, key_places, turn_a, turn_b, spread = tie(
            (
                blocks,
                up_part,
                inputs,
                grad_rows,
                query_places,
                key_places,
                turn_a,
                turn_b,
                spread,
            )
        )
        head_a, head_b, head_spread = tie((head_a, head_b, head_spread))
        up_a, up_b = up_part[:, :up_cut], up_part[:, up_cut:]
        more_a, more_b = swap_with(up_a, *order_a[2]), swap_with(up_b, *order_b[2])
        qkv_mat = blocks[:, : 3 * WIDE]
        out_mat = blocks[:, 3 * WIDE :]
        packed = blocks.reshape(owners, held, -1)[:, each, :small_len].reshape(-1)

        def widen(values):
            return round_low(dot_rows(values, spread))

        def narrow(values):
            return tail_dot(round_low(values), spread)

        def turned(values, first, second):
            return round_low(dot_rows(values, first)), round_low(dot_rows(values, second))

    else:
        small_width = -(-small_len // LANES)
        qkv_width = w_qkv.shape[0] // LANES
        blocks = jnp.concatenate(
            [w_qkv.reshape(LANES, qkv_width), pack_small(small_params, small_width)], axis=1
        )
        blocks = gather_packed(blocks, core)
        qkv_mat = blocks[..., :qkv_width].reshape(model_width, 3 * model_width)
        qkv_mat = spread_blocks(qkv_mat, model_width)
        packed = blocks[..., qkv_width:].reshape(owners, -1)[:, :small_len].reshape(-1)
        out_mat = gather_packed(w_out.reshape(LANES, -1), core).reshape(model_width, model_width)
        up_mat = gather_packed(w_up.reshape(LANES, -1), core).reshape(model_width, FF)
        down_mat = gather_packed(w_down.reshape(LANES, -1), core).reshape(FF, model_width)

        def widen(values):
            return values

        def narrow(values):
            return values

        def send_sum(left, right, extra=None):
            grad = round_low(lead_dot(left, right)).reshape(groups * 2, 2, LANES, -1)
            if extra is not None:
                extra = extra.reshape(groups * 2, 2, small_len)
                grad = jnp.concatenate([grad, pack_small(extra, small_width)], axis=-1)
            return scatter_packed(grad, core)

    packed = packed.astype(jnp.float32)
    pieces = [packed[number * model_width : (number + 1) * model_width] for number in range(7)]
    gain_one, bias_one, bias_query, bias_value, bias_out, gain_two, bias_two = pieces
    up_bias = packed[7 * model_width : 7 * model_width + FF]
    down_bias = packed[7 * model_width + FF :]

    inputs = inputs.astype(jnp.float32)
    normed_one, inverse_one = layer_stats(inputs)
    act_one = round_low(normed_one * gain_one + bias_one)
    qkv_bias = jnp.concatenate([bias_query, jnp.zeros_like(bias_query), bias_value])
    qkv_bias = spread_blocks(qkv_bias[None, :], model_width)
    own = round_low(dot_rows(widen(act_one), qkv_mat) + qkv_bias)
    other = lax.ppermute(own[:, WIDE:], "core", SWAP)
    if whole_rows:
        one_a, one_b = turned(act_one, turn_a, turn_b)
        one_a, one_b, more_a, more_b = tie((one_a, one_b, more_a, more_b))
        up_a = jnp.concatenate([up_a, more_a], axis=0)
        up_b = jnp.concatenate([up_b, more_b], axis=0)
        more_a, more_b = swap_with(up_a, *order_a[1]), swap_with(up_b, *order_b[1])
        other, one_a, one_b, up_a, up_b = tie((other, one_a, one_b, up_a, up_b))
    mixed, logs = attend(own, other, query_places, key_places)
    if whole_rows:
        mixed, more_a, more_b = tie((mixed, more_a, more_b))
        up_a = double(jnp.concatenate([up_a, more_a], axis=0), *order_a[0])
        up_b = double(jnp.concatenate([up_b, more_b], axis=0), *order_b[0])
        spread_mixed = round_low(dot_rows(mixed, head_spread))
    else:
        spread_mixed = mixed[:, :model_width]
    resid = inputs + dot_rows(spread_mixed, out_mat) + bias_out
    normed_two, inverse_two = layer_stats(resid)
    act_two = round_low(normed_two * gain_two + bias_two)
    if whole_rows:
        two_a, two_b = turned(act_two, turn_a, turn_b)
        gelu_a, slope_a = gate_and_slope(dot_rows(two_a, up_a) + up_bias[:up_cut])
        gelu_b, slope_b = gate_and_slope(dot_rows(two_b, up_b) + up_bias[up_cut:])
        slopes = [round_low(slope_a), round_low(slope_b)]
        gelu_rows = jnp.concatenate([round_low(gelu_a), round_low(gelu_b)], axis=1)
    else:
        gelu_rows, slope = gate_and_slope(dot_rows(act_two, up_mat) + up_bias)
        slopes = [round_low(slope)]
        gelu_rows = round_low(gelu_rows)
    sum_down = outer(gelu_rows, grad_rows)
    gelu_rows, sum_down, slopes = tie((gelu_rows, sum_down, slopes))
    sum_down = sum_down.reshape(owners, -1, model_width)
    sum_down = lax.psum_scatter(sum_down, ALL, scatter_dimension=0, tiled=True)

    grad_float = grad_rows.astype(jnp.float32)
    down_bias_term = jnp.sum(grad_float, axis=0)
    wide = FF // len(slopes)
    grad_pre = [
        round_low(
            tail_dot(grad_rows, down_mat[number * wide : (number + 1) * wide])
            * slope.astype(jnp.float32)
        )
        for number, slope in enumerate(slopes)
    ]
    up_bias_term = jnp.concatenate(
        [jnp.sum(part.astype(jnp.float32), axis=0) for part in grad_pre]
    )
    if whole_rows:
        pre_a, pre_b = grad_pre
        got_a = give_first(two_a, pre_a, order_a)
        got_b = give_first(two_b, pre_b, order_b)
        back_a, back_b = tail_dot(pre_a, up_a), tail_dot(pre_b, up_b)
        back_a, back_b, got_a, got_b = tie((back_a, back_b, got_a, got_b))
        sum_a = keep_first(two_a, pre_a, got_a)
        sum_b = keep_first(two_b, pre_b, got_b)
        back_a, back_b, sum_a, sum_b = tie((back_a, back_b, sum_a, sum_b))
        grad_act_two = tail_dot(round_low(back_a), turn_a) + tail_dot(round_low(back_b), turn_b)
    else:
        sum_up = send_sum(act_two, grad_pre[0])
        grad_act_two = tail_dot(grad_pre[0], up_mat)
    gain_two_term = jnp.sum(grad_act_two * normed_two, axis=0)
    bias_two_term = jnp.sum(grad_act_two, axis=0)
    grad_resid = grad_float + norm_back(grad_act_two, normed_two, inverse_two, gain_two)
    grad_attn = round_low(grad_resid)
    bias_out_term = jnp.sum(grad_attn.astype(jnp.float32), axis=0)
    grad_mixed = round_low(tail_dot(grad_attn, out_mat))
    if whole_rows:
        out_cut = (model_width // 256) * 128
        mixed_a, mixed_b = turned(mixed, head_a, head_b)
        out_got_a = give_first(mixed_a, grad_attn[:, :out_cut], order_a)
        out_got_b = give_first(mixed_b, grad_attn[:, out_cut:], order_b)
        grad_mixed = round_low(tail_dot(grad_mixed, head_spread))
        out_a = keep_first(mixed_a, grad_attn[:, :out_cut], out_got_a)
        out_b = keep_first(mixed_b, grad_attn[:, out_cut:], out_got_b)
        grad_mixed, out_a, out_b = tie((grad_mixed, out_a, out_b))
        got_a, got_b = send_half(sum_a, *order_a[1]), send_half(sum_b, *order_b[1])
        out_got_a, out_got_b = send_half(out_a, *order_a[1]), send_half(out_b, *order_b[1])
    else:
        sum_out = send_sum(mixed[:, :model_width], grad_attn)
        grad_mixed = jnp.pad(grad_mixed, [(0, 0), (0, WIDE - model_width)])
    grad_own, grad_other = attend_back(
        own, other, query_places, key_places, mixed, logs, grad_mixed
    )
    grad_got = lax.ppermute(grad_other, "core", SWAP)
    if whole_rows:
        grad_own, got_a, got_b, out_got_a, out_got_b = tie(
            (grad_own, got_a, got_b, out_got_a, out_got_b)
        )
        sum_a, sum_b = add_half(sum_a, got_a), add_half(sum_b, got_b)
        out_a, out_b = add_half(out_a, out_got_a), add_half(out_b, out_got_b)
        rest_a = jnp.concatenate([sum_a, out_a], axis=1)
        rest_b = jnp.concatenate([sum_b, out_b], axis=1)
        got_a, got_b = send_half(rest_a, *order_a[2]), send_half(rest_b, *order_b[2])
    grad_qkv_rows = add_received(grad_own, grad_got)
    if whole_rows:
        qkv_cut = (3 * WIDE // 256) * 128
        rows_a, rows_b = grad_qkv_rows[:, :qkv_cut], grad_qkv_rows[:, qkv_cut:]
        qkv_got_a = give_first(one_a, rows_a, order_a)
        qkv_got_b = give_first(one_b, rows_b, order_b)
        qkv_a = keep_first(one_a, rows_a, qkv_got_a)
        qkv_b = keep_first(one_b, rows_b, qkv_got_b)
        grad_qkv_rows, qkv_a, qkv_b, got_a, got_b, gelu_rows, sum_down = tie(
            (grad_qkv_rows, qkv_a, qkv_b, got_a, got_b, gelu_rows, sum_down)
        )
        rest = jnp.concatenate([add_half(rest_a, got_a), add_half(rest_b, got_b)], axis=1)
        qkv_got_a = send_half(qkv_a, *order_a[1])
        qkv_got_b = send_half(qkv_b, *order_b[1])
        rest_got = send_half(rest, *order_a[3])
    grad_act_one = tail_dot(grad_qkv_rows, qkv_mat)
    if whole_rows:
        grad_act_one, qkv_got_a, qkv_got_b, rest_got = tie(
            (grad_act_one, qkv_got_a, qkv_got_b, rest_got)
        )
        qkv_a, qkv_b = add_half(qkv_a, qkv_got_a), add_half(qkv_b, qkv_got_b)
        qkv_got_a = send_half(qkv_a, *order_a[2])
        qkv_got_b = send_half(qkv_b, *order_b[2])
        rest = add_half(rest, rest_got)
        rest_got = send_half(rest, *order_a[4])
    grad_act_one = narrow(grad_act_one)
    qkv_sums = jnp.sum(grad_qkv_rows.astype(jnp.float32), axis=0)
    gain_one_term = jnp.sum(grad_act_one * normed_one, axis=0)
    bias_one_term = jnp.sum(grad_act_one, axis=0)
    small_grad = jnp.concatenate(
        [
            gain_one_term,
            bias_one_term,
            qkv_sums[:model_width],
            qkv_sums[2 * WIDE : 2 * WIDE + model_width],
            bias_out_term,
            gain_two_term,
            bias_two_term,
            up_bias_term,
            down_bias_term,
        ]
    )
    small_grad = round_low(small_grad)
    grad_input = grad_resid + norm_back(grad_act_one, normed_one, inverse_one, gain_one)
    grad_input = round_low(grad_input)
    outputs = round_low(resid + dot_rows(gelu_rows, down_mat) + down_bias)
    if whole_rows:
        small_rows = round_low(lead_dot(turn_a, small_grad.reshape(model_width, -1)))
        grad_input, outputs, qkv_got_a, qkv_got_b, rest_got = tie(
            (grad_input, outputs, qkv_got_a, qkv_got_b, rest_got)
        )
        qkv_a, qkv_b = add_half(qkv_a, qkv_got_a), add_half(qkv_b, qkv_got_b)
        sum_qkv = jnp.concatenate([qkv_a, qkv_b], axis=1)
        sum_qkv = halve(sum_qkv, *order_a[3])
        rest = add_half(rest, rest_got)
        for step in order_a[5:]:
            rest = halve(rest, *step)
        for step in order_a[:4]:
            small_rows = halve(small_rows, *step)
        sum_qkv = jnp.concatenate([sum_qkv, small_rows], axis=1)
        for step in order_a[4:]:
            sum_qkv = halve(sum_qkv, *step)
        sides = [up_cut, up_cut + out_cut, FF + out_cut]
        sum_up = jnp.concatenate([rest[:, : sides[0]], rest[:, sides[1] : sides[2]]], axis=1)
        sum_out = jnp.concatenate([rest[:, sides[0] : sides[1]], rest[:, sides[2] :]], axis=1)
        grad_qkv = pick_blocks(sum_qkv, model_width)
        grad_small = sum_qkv[:, 3 * WIDE :]
    else:
        sum_qkv = send_sum(act_one, pick_blocks(grad_qkv_rows, model_width), small_grad)
        grad_qkv, grad_small = sum_qkv[:, :qkv_width], sum_qkv[:, qkv_width:]
    result = trade_back(outputs)
    grad_tokens = trade_back(grad_input)
    grad_small = grad_small.astype(jnp.float32).reshape(-1)[:small_len]
    grad_qkv, grad_out, grad_up, grad_down = [
        piece.astype(jnp.float32).reshape(-1) for piece in (grad_qkv, sum_out, sum_up, sum_down)
    ]
    return (result, grad_tokens, grad_qkv, grad_out, grad_up, grad_down, grad_small)


def solution(mesh):
    groups, owners = mesh.shape["dp"], mesh.shape["ctx"]
    fine = Mesh(mesh.devices.reshape(groups, owners // 2, 2), ("dp", "y", "core"))
    rows = P("dp", ("y", "core"), None)
    flat = P(("dp", "y", "core"))
    return jax.shard_map(
        local,
        mesh=fine,
        in_specs=(rows, P("dp", None), flat, flat, flat, flat, flat, rows),
        out_specs=(rows, rows, flat, flat, flat, flat, flat),
        check_vma=False,
    )
```

profile of v0, /device:TPU:0, one launch (start us, length us, event | category | flops | bytes accessed | tf_op | source)
XLA Modules:
  0.0 577.4 jit_solution(3582670324101781780)
XLA Ops:
  49.4 19.5 %collective-permute-done.1 = bf16[68,4352]{1,0:T(8,128)(2,1)} collective-permute-done((bf16[68,4352]{1,0:T(8,128)(2,1)}, bf16[68,4352]{1,0:T(8,128)(2,1)}, u32[]{:S(2)}, u32[]{:S(2)}) %collective-permute-start.1) | collective-permute-done | bytes 591904 | tf_op jit(solution)/shard_map/ppermute | solution.py:332
  70.2 47.6 %all-gather.3.cloned.1.call-done = bf16[1280,4544]{1,0:T(8,128)(2,1)} async-done(((bf16[40,4544]{1,0:T(8,128)(2,1)}), bf16[1280,4544]{1,0:T(8,128)(2,1)}) %all-gather.3.cloned.1.call-update) | async-done | bytes 11632656 | tf_op jit(solution)/shard_map/all_gather | solution.py:462
  129.5 13.1 %add_convert_fusion.own_ref = bf16[512,3456]{1,0:T(8,128)(2,1)} fusion(bf16[1280,4544]{1,0:T(8,128)(2,1)} %all-gather.3.cloned.1.call-done, f32[3456]{0:T(1024)S(1)} %reduce.6, bf16[1088,1280]{1,0:T(8,128)(2,1)} %fusion.7, bf16[512,1088]{1,0:T(8,128)(2,1)S(1)} %pad_maximum_fusion.6, f32[1088]{0:T(1024)S(1)} %copy-done.85, f32[1088]{0:T(1024)S(1)} %get-tuple-element.216, ...), kind=kOutput, calls=%fused_computation.4 | convolution fusion | flops 5963448320 | bytes 16312320 | tf_op jit(solution)/shard_map/dot_general | solution.py:78
  166.3 19.2 %shard_map.135 = (bf16[512,1152]{1,0:T(8,128)(2,1)S(1)}, f32[17,512]{1,0:T(8,128)S(1)}) custom-call(bf16[512,3456]{1,0:T(8,128)(2,1)} %add_convert_fusion.own_ref, bf16[512,2304]{1,0:T(8,128)(2,1)S(1)} %collective-permute-done.4.other_ref, s32[1,512]{1,0:T(1,128)S(1)} %bitcast.87, s32[1024,1]{1,0:T(8,128)S(1)} %copy-done.4), custom_call_target="tpu_custom_call" | custom-call | flops 1073741824 | bytes 12582912 | tf_op jit(solution)/shard_map/pallas_call | solution.py:306
  185.5 9.5 %collective-permute-done.8 = bf16[272,2176]{1,0:T(8,128)(2,1)} collective-permute-done((bf16[272,2176]{1,0:T(8,128)(2,1)}, bf16[272,2176]{1,0:T(8,128)(2,1)}, u32[]{:S(2)}, u32[]{:S(2)}) %collective-permute-start.8) | collective-permute-done | bytes 1183776 | tf_op jit(solution)/shard_map/ppermute | solution.py:332
  195.1 7.3 %collective-permute-done.7 = bf16[272,2176]{1,0:T(8,128)(2,1)} collective-permute-done((bf16[272,2176]{1,0:T(8,128)(2,1)}, bf16[272,2176]{1,0:T(8,128)(2,1)}, u32[]{:S(2)}, u32[]{:S(2)}) %collective-permute-start.7) | collective-permute-done | bytes 1183776 | tf_op jit(solution)/shard_map/ppermute | solution.py:332
  209.5 8.6 %fusion.115 = (f32[512]{0:T(512)}, f32[512,1088]{1,0:T(8,128)}) fusion(f32[1088]{0:T(1024)S(1)} %copy-done.84, bf16[1280,4544]{1,0:T(8,128)(2,1)} %all-gather.3.cloned.1.call-done, bf16[512,1152]{1,0:T(8,128)(2,1)S(1)} %copy-done.7, bf16[1152,1280]{1,0:T(8,128)(2,1)} %fusion.6, bf16[512,1088]{1,0:T(8,128)(2,1)S(1)} %copy-done.12), kind=kOutput, calls=%fused_computation.269 | convolution fusion | flops 2938895872 | bytes 10426624 | tf_op jit(solution)/shard_map/dot_general | solution.py:78
  238.8 7.1 %add_convert_fusion.4 = (bf16[512,2176]{1,0:T(8,128)(2,1)}, bf16[512,2176]{1,0:T(8,128)(2,1)S(1)}) fusion(f32[2176]{0:T(1024)S(1)} %copy-done.79, bf16[512,1088]{0,1:T(8,128)(2,1)S(1)} %convolution_convert_fusion.13, bf16[1088,2176]{1,0:T(8,128)(2,1)S(1)} %constant_dynamic-update-slice_fusion.1), kind=kOutput, calls=%fused_computation.33 | convolution fusion | flops 2446589952 | bytes 10314240 | tf_op jit(solution)/shard_map/dot_general | solution.py:78
  245.9 7.0 %add_convert_fusion.3 = (bf16[512,2176]{1,0:T(8,128)(2,1)}, bf16[512,2176]{1,0:T(8,128)(2,1)S(1)}) fusion(f32[2176]{0:T(1024)S(1)} %copy-done.78, bf16[512,1088]{0,1:T(8,128)(2,1)S(1)} %convolution_convert_fusion.12, bf16[1088,2176]{1,0:T(8,128)(2,1)S(1)} %constant_dynamic-update-slice_fusion.4), kind=kOutput, calls=%fused_computation.32 | convolution fusion | flops 2446589952 | bytes 10314240 | tf_op jit(solution)/shard_map/dot_general | solution.py:78
  253.1 9.6 %shard_map.136 = bf16[4352,1088]{1,0:T(8,128)(2,1)S(1)} custom-call(bf16[512,4352]{1,0:T(8,128)(2,1)S(1)} %pad_maximum_fusion.left_ref, bf16[512,1088]{1,0:T(8,128)(2,1)S(1)} %pad_maximum_fusion.7.right_ref), custom_call_target="tpu_custom_call" | custom-call | flops 4848615424 | bytes 16777216 | tf_op jit(solution)/shard_map/pallas_call | solution.py:283
  266.6 7.0 %fusion.118 = (bf16[2176]{0:T(1024)(128)(2,1)}, bf16[512,2176]{1,0:T(8,128)(2,1)S(1)}) fusion(bf16[512,2176]{1,0:T(8,128)(2,1)} %get-tuple-element.93, bf16[512,1088]{1,0:T(8,128)(2,1)S(1)} %pad_maximum_fusion.7.right_ref, bf16[4352,1088]{1,0:T(8,128)(2,1)} %all-gather.5.cloned.1.call-done), kind=kOutput, calls=%fused_computation.272 | convolution fusion | flops 2428762112 | bytes 10588416 | tf_op jit(solution)/shard_map/dot_general | solution.py:39
  291.5 5.2 fusion.119
  322.2 6.6 %convolution_convert_fusion.10.grad_ref = bf16[512,1152]{1,0:T(8,128)(2,1)S(1)} fusion(bf16[1152,1280]{1,0:T(8,128)(2,1)} %fusion.6, bf16[512,1088]{1,0:T(8,128)(2,1)S(1)} %get-tuple-element.164, bf16[1280,4544]{1,0:T(8,128)(2,1)} %all-gather.3.cloned.1.call-done), kind=kOutput, calls=%fused_computation.55 | convolution fusion | flops 2937257984 | bytes 8192000 | tf_op jit(solution)/shard_map/dot_general | solution.py:39
  337.8 27.3 %shard_map.137 = (bf16[512,3456]{1,0:T(8,128)(2,1)}, bf16[512,2304]{1,0:T(8,128)(2,1)}) custom-call(bf16[512,3456]{1,0:T(8,128)(2,1)} %add_convert_fusion.own_ref, bf16[512,2304]{1,0:T(8,128)(2,1)} %copy-done.3, s32[1,512]{1,0:T(1,128)S(1)} %bitcast.88, s32[1024,1]{1,0:T(8,128)S(1)} %copy-done.5, bf16[512,1152]{1,0:T(8,128)(2,1)S(1)} %copy-done.7, ...), custom_call_target="tpu_custom_call" | custom-call | flops 1073741824 | bytes 12582912 | tf_op jit(solution)/shard_map/pallas_call | solution.py:315
  367.1 16.8 %collective-permute-done.17 = bf16[272,512]{1,0:T(8,128)(2,1)S(1)} collective-permute-done((bf16[272,512]{1,0:T(8,128)(2,1)S(1)}, bf16[272,512]{1,0:T(8,128)(2,1)S(1)}, u32[]{:S(2)}, u32[]{:S(2)}) %collective-permute-start.17) | collective-permute-done | bytes 278560 | tf_op jit(solution)/shard_map/ppermute | solution.py:332
  406.5 14.7 %collective-permute-done.22 = bf16[136,2688]{1,0:T(8,128)(2,1)S(1)} collective-permute-done((bf16[136,2688]{1,0:T(8,128)(2,1)S(1)}, bf16[136,2688]{1,0:T(8,128)(2,1)S(1)}, u32[]{:S(2)}, u32[]{:S(2)}) %collective-permute-start.22) | collective-permute-done | bytes 731168 | tf_op jit(solution)/shard_map/ppermute | solution.py:332
  422.1 21.7 %reduce-scatter.4.cloned.1.call-done = bf16[1,136,1088]{2,1,0:T(8,128)(2,1)} async-done(((bf16[32,136,1088]{2,1,0:T(8,128)(2,1)}), bf16[1,136,1088]{2,1,0:T(8,128)(2,1)}) %reduce-scatter.4.cloned.1.call-update) | async-done | bytes 295952 | tf_op jit(solution)/shard_map/optimization_barrier | solution.py:637
  443.8 8.8 %fusion = bf16[512,1280]{1,0:T(8,128)(2,1)} fusion(bf16[512,3456]{1,0:T(8,128)(2,1)S(1)} %shard_map.138, bf16[1280,4544]{1,0:T(8,128)(2,1)} %all-gather.3.cloned.1.call-done), kind=kOutput, calls=%fused_computation | convolution fusion | flops 4529848320 | bytes 13697024 | tf_op jit(solution)/shard_map/dot_general | solution.py:39
  462.7 11.8 %fusion.22 = bf16[512,1088]{1,0:T(8,128)(2,1)} fusion(f32[512,1088]{1,0:T(8,128)S(1)} %copy-done.23, bf16[512,4352]{1,0:T(8,128)(2,1)} %copy-done.2, bf16[4352,1088]{1,0:T(8,128)(2,1)} %all-gather.5.cloned.1.call-done, f32[1088]{0:T(1024)S(1)} %copy-done.82), kind=kOutput, calls=%fused_computation.63 | convolution fusion | flops 4850286592 | bytes 17273088 | tf_op jit(solution)/shard_map/dot_general | solution.py:78
  494.7 7.5 %concatenate.123 = bf16[13056]{0:T(1024)(128)(2,1)} concatenate(bf16[1088]{0:T(1024)(128)(2,1)} %get-tuple-element.158, bf16[1088]{0:T(1024)(128)(2,1)} %get-tuple-element.227, bf16[1088]{0:T(1024)(128)(2,1)} %get-tuple-element.223, bf16[1088]{0:T(1024)(128)(2,1)} %get-tuple-element.222, bf16[1088]{0:T(1024)(128)(2,1)} %get-tuple-element.163, ...), dimensions={0} | concatenate | bytes 52224 | tf_op jit(solution)/shard_map/concatenate | solution.py:658
  513.8 12.2 %collective-permute-done.34 = bf16[272,12]{1,0:T(8,128)(2,1)S(1)} collective-permute-done((bf16[272,12]{1,0:T(8,128)(2,1)S(1)}, bf16[272,12]{1,0:T(8,128)(2,1)S(1)}, u32[]{:S(2)}, u32[]{:S(2)}) %collective-permute-start.34) | collective-permute-done | bytes 6560 | tf_op jit(solution)/shard_map/ppermute | solution.py:332
  544.9 5.2 collective-permute-done.32
  552.2 5.4 collective-permute-done.30
  560.7 4.8 collective-permute-done.31
  (475 shorter events, 258.3 us)
Async XLA Ops:
  7.2 110.6 %all-gather.3.cloned.1.call-start = ((), (), s32[]{:S(2)}) async-start(), calls=%async_computation.1 | async-start | bytes 12165120 | tf_op jit(solution)/shard_map/all_gather | solution.py:462
  11.3 255.2 %all-gather.5.cloned.1.call-start = ((), (), s32[]{:S(2)}) async-start(), calls=%async_computation.2 | async-start | bytes 10340352 | tf_op jit(solution)/shard_map/all_gather | solution.py:463
  11.8 27.3 %collective-permute-start = (bf16[34,4352]{1,0:T(8,128)(2,1)S(1)}, bf16[34,4352]{1,0:T(8,128)(2,1)S(1)}, u32[]{:S(2)}, u32[]{:S(2)}) collective-permute-start(bf16[34,4352]{1,0:T(8,128)(2,1)S(1)} %reshape.202), channel_id=1, source_target_pairs={{0,16},{4,20},{8,24},{12,28},{16,0},{20,4},{24,8},{28,12},{1,17},{... | collective-permute-start | bytes 887816 | tf_op jit(solution)/shard_map/ppermute | solution.py:332
  16.7 24.3 %collective-permute-start.3 = (bf16[256,1088]{0,1:T(8,128)(2,1)}, bf16[256,1088]{0,1:T(8,128)(2,1)}, u32[]{:S(2)}, u32[]{:S(2)}) collective-permute-start(bf16[256,1088]{0,1:T(8,128)(2,1)} %dynamic-slice_bitcast_fusion), channel_id=1, source_target_pairs={{0,2},{2,0},{1,3},{3,1},{4,6},{6,4},{5,7},{7,5},{8,10},{10,8},{9,1... | collective-permute-start | bytes 1671176 | tf_op jit(solution)/shard_map/ppermute | solution.py:409
  19.1 26.6 %collective-permute-start.2 = (bf16[256,1088]{0,1:T(8,128)(2,1)}, bf16[256,1088]{0,1:T(8,128)(2,1)}, u32[]{:S(2)}, u32[]{:S(2)}) collective-permute-start(bf16[256,1088]{0,1:T(8,128)(2,1)} %dynamic-slice_bitcast_fusion.1), channel_id=1, source_target_pairs={{0,2},{2,0},{1,3},{3,1},{4,6},{6,4},{5,7},{7,5},{8,10},{10,8},{9,1... | collective-permute-start | bytes 1671176 | tf_op jit(solution)/shard_map/ppermute | solution.py:409
  20.6 423.2 %reduce-scatter.4.cloned.1.call-start = ((), (), s32[]{:S(2)}) async-start(), calls=%async_computation.3 | async-start | bytes 10340352
  40.0 28.8 %collective-permute-start.1 = (bf16[68,4352]{1,0:T(8,128)(2,1)}, bf16[68,4352]{1,0:T(8,128)(2,1)}, u32[]{:S(2)}, u32[]{:S(2)}) collective-permute-start(bf16[68,4352]{1,0:T(8,128)(2,1)} %pad_maximum_fusion.13), channel_id=1, source_target_pairs={{0,8},{4,12},{8,0},{12,4},{16,24},{20,28},{24,16},{28,20},{1,9},{5... | collective-permute-start | bytes 1775624 | tf_op jit(solution)/shard_map/ppermute | solution.py:332
  126.5 26.6 %collective-permute-start.6 = (bf16[136,2176]{1,0:T(8,128)(2,1)}, bf16[136,2176]{1,0:T(8,128)(2,1)}, u32[]{:S(2)}, u32[]{:S(2)}) collective-permute-start(bf16[136,2176]{1,0:T(8,128)(2,1)} %get-tuple-element.178), channel_id=1, source_target_pairs={{0,4},{4,0},{8,12},{12,8},{16,20},{20,16},{24,28},{28,24},{1,5},{5... | collective-permute-start | bytes 1775624 | tf_op jit(solution)/shard_map/ppermute | solution.py:332
  127.9 25.2 %collective-permute-start.5 = (bf16[136,2176]{1,0:T(8,128)(2,1)}, bf16[136,2176]{1,0:T(8,128)(2,1)}, u32[]{:S(2)}, u32[]{:S(2)}) collective-permute-start(bf16[136,2176]{1,0:T(8,128)(2,1)} %get-tuple-element.179), channel_id=1, source_target_pairs={{0,2},{2,0},{1,3},{3,1},{4,6},{6,4},{5,7},{7,5},{8,10},{10,8},{9,1... | collective-permute-start | bytes 1775624 | tf_op jit(solution)/shard_map/ppermute | solution.py:332
  155.5 39.5 %collective-permute-start.8 = (bf16[272,2176]{1,0:T(8,128)(2,1)}, bf16[272,2176]{1,0:T(8,128)(2,1)}, u32[]{:S(2)}, u32[]{:S(2)}) collective-permute-start(bf16[272,2176]{1,0:T(8,128)(2,1)} %pad_maximum_fusion.5), channel_id=1, source_target_pairs={{0,2},{2,0},{1,3},{3,1},{4,6},{6,4},{5,7},{7,5},{8,10},{10,8},{9,1... | collective-permute-start | bytes 3551240 | tf_op jit(solution)/shard_map/ppermute | solution.py:332
  159.3 43.1 %collective-permute-start.7 = (bf16[272,2176]{1,0:T(8,128)(2,1)}, bf16[272,2176]{1,0:T(8,128)(2,1)}, u32[]{:S(2)}, u32[]{:S(2)}) collective-permute-start(bf16[272,2176]{1,0:T(8,128)(2,1)} %pad_maximum_fusion.4), channel_id=1, source_target_pairs={{0,4},{4,0},{8,12},{12,8},{16,20},{20,16},{24,28},{28,24},{1,5},{5... | collective-permute-start | bytes 3551240 | tf_op jit(solution)/shard_map/ppermute | solution.py:332
  205.6 27.4 %collective-permute-start.10 = (bf16[544,2176]{1,0:T(8,128)(2,1)}, bf16[544,2176]{1,0:T(8,128)(2,1)}, u32[]{:S(2)}, u32[]{:S(2)}) collective-permute-start(bf16[544,2176]{1,0:T(8,128)(2,1)} %pad_maximum_fusion.2), channel_id=1, source_target_pairs={{0,1},{1,0},{2,3},{3,2},{4,5},{5,4},{6,7},{7,6},{8,9},{9,8},{10,11... | collective-permute-start | bytes 7102472 | tf_op jit(solution)/shard_map/ppermute | solution.py:332
  209.2 25.9 %collective-permute-start.9 = (bf16[544,2176]{1,0:T(8,128)(2,1)}, bf16[544,2176]{1,0:T(8,128)(2,1)}, u32[]{:S(2)}, u32[]{:S(2)}) collective-permute-start(bf16[544,2176]{1,0:T(8,128)(2,1)} %pad_maximum_fusion.1), channel_id=1, source_target_pairs={{0,1},{1,0},{2,3},{3,2},{4,5},{5,4},{6,7},{7,6},{8,9},{9,8},{10,11... | collective-permute-start | bytes 7102472 | tf_op jit(solution)/shard_map/ppermute | solution.py:332
  332.0 53.8 %collective-permute-start.16 = (bf16[272,2176]{1,0:T(8,128)(2,1)}, bf16[272,2176]{1,0:T(8,128)(2,1)}, u32[]{:S(2)}, u32[]{:S(2)}) collective-permute-start(bf16[272,2176]{1,0:T(8,128)(2,1)} %slice.435), channel_id=1, source_target_pairs={{0,2},{2,0},{1,3},{3,1},{4,6},{6,4},{5,7},{7,5},{8,10},{10,8},{9,1... | collective-permute-start | bytes 3551240 | tf_op jit(solution)/shard_map/ppermute | solution.py:332
  332.0 53.8 %collective-permute-start.15 = (bf16[272,2176]{1,0:T(8,128)(2,1)S(1)}, bf16[272,2176]{1,0:T(8,128)(2,1)}, u32[]{:S(2)}, u32[]{:S(2)}) collective-permute-start(bf16[272,2176]{1,0:T(8,128)(2,1)S(1)} %slice.434), channel_id=1, source_target_pairs={{0,4},{4,0},{8,12},{12,8},{16,20},{20,16},{24,28},{28,24},{1,5},{5... | collective-permute-start | bytes 3551240 | tf_op jit(solution)/shard_map/ppermute | solution.py:332
  365.0 26.4 %collective-permute-start.19 = (bf16[512,2304]{1,0:T(8,128)(2,1)}, bf16[512,2304]{1,0:T(8,128)(2,1)}, u32[]{:S(2)}, u32[]{:S(2)}) collective-permute-start(bf16[512,2304]{1,0:T(8,128)(2,1)} %get-tuple-element.110), channel_id=1, source_target_pairs={{0,1},{1,0},{2,3},{3,2},{4,5},{5,4},{6,7},{7,6},{8,9},{9,8},{10,11... | collective-permute-start | bytes 7077896 | tf_op jit(solution)/shard_map/ppermute | solution.py:619
  397.4 23.8 %collective-permute-start.22 = (bf16[136,2688]{1,0:T(8,128)(2,1)S(1)}, bf16[136,2688]{1,0:T(8,128)(2,1)S(1)}, u32[]{:S(2)}, u32[]{:S(2)}) collective-permute-start(bf16[136,2688]{1,0:T(8,128)(2,1)S(1)} %fusion.53), channel_id=1, source_target_pairs={{0,2},{2,0},{1,3},{3,1},{4,6},{6,4},{5,7},{7,5},{8,10},{10,8},{9,1... | collective-permute-start | bytes 2193416 | tf_op jit(solution)/shard_map/ppermute | solution.py:332
  398.9 23.2 %collective-permute-start.23 = (bf16[136,2752]{1,0:T(8,128)(2,1)S(1)}, bf16[136,2752]{1,0:T(8,128)(2,1)}, u32[]{:S(2)}, u32[]{:S(2)}) collective-permute-start(bf16[136,2752]{1,0:T(8,128)(2,1)S(1)} %fusion.51), channel_id=1, source_target_pairs={{0,4},{4,0},{8,12},{12,8},{16,20},{20,16},{24,28},{28,24},{1,5},{5... | collective-permute-start | bytes 2245640 | tf_op jit(solution)/shard_map/ppermute | solution.py:332
  456.7 21.2 %collective-permute-start.26 = (bf16[68,5440]{1,0:T(8,128)(2,1)}, bf16[68,5440]{1,0:T(8,128)(2,1)}, u32[]{:S(2)}, u32[]{:S(2)}) collective-permute-start(bf16[68,5440]{1,0:T(8,128)(2,1)} %fusion.50), channel_id=1, source_target_pairs={{0,8},{4,12},{8,0},{12,4},{16,24},{20,28},{24,16},{28,20},{1,9},{5... | collective-permute-start | bytes 2219528 | tf_op jit(solution)/shard_map/ppermute | solution.py:332
  461.3 21.3 %collective-permute-start.25 = (bf16[272,1792]{1,0:T(8,128)(2,1)}, bf16[272,1792]{1,0:T(8,128)(2,1)}, u32[]{:S(2)}, u32[]{:S(2)}) collective-permute-start(bf16[272,1792]{1,0:T(8,128)(2,1)} %slice.451), channel_id=1, source_target_pairs={{0,2},{2,0},{1,3},{3,1},{4,6},{6,4},{5,7},{7,5},{8,10},{10,8},{9,1... | collective-permute-start | bytes 2924552 | tf_op jit(solution)/shard_map/ppermute | solution.py:332
  508.9 25.1 %collective-permute-start.29 = (bf16[34,5440]{1,0:T(8,128)(2,1)S(1)}, bf16[34,5440]{1,0:T(8,128)(2,1)S(1)}, u32[]{:S(2)}, u32[]{:S(2)}) collective-permute-start(bf16[34,5440]{1,0:T(8,128)(2,1)S(1)} %slice.539), channel_id=1, source_target_pairs={{0,16},{4,20},{8,24},{12,28},{16,0},{20,4},{24,8},{28,12},{1,17},{... | collective-permute-start | bytes 1109768 | tf_op jit(solution)/shard_map/ppermute | solution.py:332
  510.6 23.4 %collective-permute-start.27 = (bf16[136,1664]{1,0:T(8,128)(2,1)S(1)}, bf16[136,1664]{1,0:T(8,128)(2,1)S(1)}, u32[]{:S(2)}, u32[]{:S(2)}) collective-permute-start(bf16[136,1664]{1,0:T(8,128)(2,1)S(1)} %slice.537), channel_id=1, source_target_pairs={{0,2},{2,0},{1,3},{3,1},{4,6},{6,4},{5,7},{7,5},{8,10},{10,8},{9,1... | collective-permute-start | bytes 1357832 | tf_op jit(solution)/shard_map/ppermute | solution.py:332
  511.6 22.3 %collective-permute-start.28 = (bf16[136,1792]{1,0:T(8,128)(2,1)S(1)}, bf16[136,1792]{1,0:T(8,128)(2,1)S(1)}, u32[]{:S(2)}, u32[]{:S(2)}) collective-permute-start(bf16[136,1792]{1,0:T(8,128)(2,1)S(1)} %slice.538), channel_id=1, source_target_pairs={{0,4},{4,0},{8,12},{12,8},{16,20},{20,16},{24,28},{28,24},{1,5},{5... | collective-permute-start | bytes 1462280 | tf_op jit(solution)/shard_map/ppermute | solution.py:332
  543.9 21.5 %collective-permute-start.31 = (bf16[256,1088]{0,1:T(8,128)(2,1)}, bf16[256,1088]{0,1:T(8,128)(2,1)}, u32[]{:S(2)}, u32[]{:S(2)}) collective-permute-start(bf16[256,1088]{0,1:T(8,128)(2,1)} %copy.60), channel_id=1, source_target_pairs={{0,2},{2,0},{1,3},{3,1},{4,6},{6,4},{5,7},{7,5},{8,10},{10,8},{9,1... | collective-permute-start | bytes 1671176 | tf_op jit(solution)/shard_map/ppermute | solution.py:415
  (127 other events, 1178.3 us)
Sparse Core Ops, SparseCore 0:
  11.5 106.2 all-gather.2
  120.6 98.4 all-gather.4
  288.2 155.6 reduce-scatter.3
where the time goes:
time: 589 us; the launch traced here: 577 us
  waiting for transfers between devices  180 us (31%)
  matrix products  132 us (22%)
  local copies, waits for them, and re-layouts  82.8 us (14%)
  other arithmetic  74.3 us (13%)
  Pallas kernels  58.3 us (10%)
  starting transfers between devices  34.4 us (6%)
  between operations  15.7 us (3%)
    ppermute x32, waiting for transfers between devices, swap_with(): lax.ppermute(values, axis, [(here, here ^ 1 << bit) for here in range(cou...  96.8 us
    dot_general x11, matrix products, dot_rows(): lax.dot_general(left, right, (((1,), (0,)), ((), ())), preferred_element_...  64 us
    all_gather x1, waiting for transfers between devices, local(): blocks = lax.all_gather(blocks, ALL, axis=0, tiled=True)  47.6 us
    dot_general x9, matrix products, tail_dot(): lax.dot_general(left_side, right_side, (((1,), (1,)), ((), ())), preferre...  43.9 us
    ppermute x32, starting transfers between devices, swap_with(): lax.ppermute(values, axis, [(here, here ^ 1 << bit) for here in range(cou...  30.2 us
    convert_element_type x23, other arithmetic, round_low(): return values.astype(jnp.bfloat16)  28.6 us
    unnamed x241, local copies, waits for them, and re-layouts  27.7 us
    pallas_call x1, Pallas kernels, attend_back(): return call(own, other, query_places, key_places, mixed, logs, grad)  27.3 us
  transfers between devices with their start and end apart: 41, of which 18 were waited for; matrix products, arithmetic and copies ran while one was open for 37% of the time, Pallas kernels for 10%

commit v1 on v0

--- a/solution.py
+++ b/solution.py
@@ -272,14 +272,18 @@
     )
 
 
-def outer_kernel(left_ref, right_ref, out_ref):
-    out_ref[...] = lead_dot(left_ref[...], right_ref[...]).astype(out_ref.dtype)
+def outer_kernel(left_ref, right_ref, first_ref, second_ref):
+    part = lead_dot(left_ref[...], right_ref[...]).astype(first_ref.dtype)
+    cut = first_ref.shape[1]
+    first_ref[...] = part[:, :cut]
+    second_ref[...] = part[:, cut:]
 
 
 def outer(left, right):
     rows, count = left.shape
     width = right.shape[1]
     step = 256
+    cut = (width // 256) * 128
     return pl.pallas_call(
         outer_kernel,
         grid=(count // step,),
@@ -287,8 +291,14 @@
             pl.BlockSpec((rows, step), lambda i: (0, i)),
             pl.BlockSpec((rows, width), lambda i: (0, 0)),
         ],
-        out_specs=pl.BlockSpec((step, width), lambda i: (i, 0)),
-        out_shape=jax.ShapeDtypeStruct((count, width), jnp.bfloat16),
+        out_specs=[
+            pl.BlockSpec((step, cut), lambda i: (i, 0)),
+            pl.BlockSpec((step, width - cut), lambda i: (i, 0)),
+        ],
+        out_shape=[
+            jax.ShapeDtypeStruct((count, cut), jnp.bfloat16),
+            jax.ShapeDtypeStruct((count, width - cut), jnp.bfloat16),
+        ],
         compiler_params=pltpu.CompilerParams(vmem_limit_bytes=32 * 1024 * 1024),
         cost_estimate=pl.CostEstimate(
             flops=2 * rows * count * width, bytes_accessed=16 << 20, transcendentals=0
@@ -296,13 +306,119 @@
     )(left, right)
 
 
+def input_grad_kernel(
+    rows_ref,
+    mat_ref,
+    spread_ref,
+    input_ref,
+    gain_ref,
+    resid_ref,
+    out_ref,
+    gain_out,
+    bias_out,
+    total,
+):
+    step = pl.program_id(0)
+    part = tail_dot(rows_ref[...], mat_ref[...])
+
+    @pl.when(step == 0)
+    def _():
+        total[...] = part
+
+    @pl.when(step > 0)
+    def _():
+        total[...] += part
+
+    @pl.when(step == pl.num_programs(0) - 1)
+    def _():
+        back = tail_dot(total[...].astype(jnp.bfloat16), spread_ref[...])
+        normed, inverse = layer_stats(input_ref[...].astype(jnp.float32))
+        gain_out[...] = jnp.sum(back * normed, axis=0, keepdims=True)
+        bias_out[...] = jnp.sum(back, axis=0, keepdims=True)
+        grad = resid_ref[...] + norm_back(back, normed, inverse, gain_ref[...])
+        out_ref[...] = grad.astype(out_ref.dtype)
+
+
+def input_grad(rows, mat, spread, inputs, gain, resid):
+    count, width = inputs.shape
+    held = mat.shape[0]
+    step = 384
+
+    def fixed(shape):
+        return pl.BlockSpec(shape, lambda i: (0, 0))
+
+    return pl.pallas_call(
+        input_grad_kernel,
+        grid=(3 * WIDE // step,),
+        in_specs=[
+            pl.BlockSpec((count, step), lambda i: (0, i)),
+            pl.BlockSpec((held, step), lambda i: (0, i)),
+            fixed((width, held)),
+            fixed((count, width)),
+            fixed((1, width)),
+            fixed((count, width)),
+        ],
+        out_specs=[fixed((count, width)), fixed((1, width)), fixed((1, width))],
+        out_shape=[
+            jax.ShapeDtypeStruct((count, width), jnp.bfloat16),
+            jax.ShapeDtypeStruct((1, width), jnp.float32),
+            jax.ShapeDtypeStruct((1, width), jnp.float32),
+        ],
+        scratch_shapes=[pltpu.VMEM((count, held), jnp.float32)],
+        compiler_params=pltpu.CompilerParams(vmem_limit_bytes=48 * 1024 * 1024),
+        cost_estimate=pl.CostEstimate(flops=14 << 30, bytes_accessed=20 << 20, transcendentals=0),
+    )(rows, mat, spread, inputs, gain, resid)
+
+
+def project_kernel(left_ref, mat_ref, resid_ref, bias_ref, out_ref, total):
+    step = pl.program_id(0)
+    part = dot_rows(left_ref[...], mat_ref[...])
+
+    @pl.when(step == 0)
+    def _():
+        total[...] = resid_ref[...] + bias_ref[...] + part
+
+    @pl.when(step > 0)
+    def _():
+        total[...] += part
+
+    @pl.when(step == pl.num_programs(0) - 1)
+    def _():
+        out_ref[...] = total[...].astype(out_ref.dtype)
+
+
+def project(left, mat, resid, bias):
+    count, depth = left.shape
+    width = mat.shape[1]
+    step = 256
+
+    def fixed(shape):
+        return pl.BlockSpec(shape, lambda i: (0, 0))
+
+    return pl.pallas_call(
+        project_kernel,
+        grid=(depth // step,),
+        in_specs=[
+            pl.BlockSpec((count, step), lambda i: (0, i)),
+            pl.BlockSpec((step, width), lambda i: (i, 0)),
+            fixed((count, width)),
+            fixed((1, width)),
+        ],
+        out_specs=fixed((count, width)),
+        out_shape=jax.ShapeDtypeStruct((count, width), jnp.bfloat16),
+        scratch_shapes=[pltpu.VMEM((count, width), jnp.float32)],
+        compiler_params=pltpu.CompilerParams(vmem_limit_bytes=32 * 1024 * 1024),
+        cost_estimate=pl.CostEstimate(flops=14 << 30, bytes_accessed=20 << 20, transcendentals=0),
+    )(left, mat, resid, bias)
+
+
 def attend(own, other, query_places, key_places):
     rows = own.shape[0]
     outs = (
         jax.ShapeDtypeStruct((rows, WIDE), jnp.bfloat16),
         jax.ShapeDtypeStruct((HEADS, rows), jnp.float32),
     )
-    call = kernel_call(attend_kernel, outs, rows // 2, 1 << 30)
+    call = kernel_call(attend_kernel, outs, rows // 2, 20 << 30)
     return call(own, other, query_places, key_places)
 
 
@@ -311,7 +427,7 @@
         jax.ShapeDtypeStruct(own.shape, jnp.bfloat16),
         jax.ShapeDtypeStruct(other.shape, jnp.bfloat16),
     )
-    call = kernel_call(attend_back_kernel, outs, own.shape[0] // 2, 1 << 30)
+    call = kernel_call(attend_back_kernel, outs, own.shape[0] // 2, 30 << 30)
     return call(own, other, query_places, key_places, mixed, logs, grad)
 
 
@@ -409,10 +525,13 @@
         got = lax.ppermute(give, "y", SWAP)
         return jnp.concatenate([mine[:span], got[:span], mine[span:], got[span:]], axis=0)
 
-    def trade_back(values):
+    def trade_out(values):
+        return lax.ppermute(
+            jnp.concatenate([values[span:half], values[half + span :]], axis=0), "y", SWAP
+        )
+
+    def trade_join(values, got):
         mine = jnp.concatenate([values[:span], values[half : half + span]], axis=0)
-        give = jnp.concatenate([values[span:half], values[half + span :]], axis=0)
-        got = lax.ppermute(give, "y", SWAP)
         first = jnp.where(y == 0, mine, got)
         second = jnp.where(y == 0, got, mine)
         return jnp.stack([first, second])
@@ -481,15 +600,13 @@
         head_a, head_b, head_spread = tie((head_a, head_b, head_spread))
         up_a, up_b = up_part[:, :up_cut], up_part[:, up_cut:]
         more_a, more_b = swap_with(up_a, *order_a[2]), swap_with(up_b, *order_b[2])
+        grad_mat = blocks
         qkv_mat = blocks[:, : 3 * WIDE]
         out_mat = blocks[:, 3 * WIDE :]
         packed = blocks.reshape(owners, held, -1)[:, each, :small_len].reshape(-1)
 
         def widen(values):
             return round_low(dot_rows(values, spread))
-
-        def narrow(values):
-            return tail_dot(round_low(values), spread)
 
         def turned(values, first, second):
             return round_low(dot_rows(values, first)), round_low(dot_rows(values, second))
@@ -503,15 +620,15 @@
         blocks = gather_packed(blocks, core)
         qkv_mat = blocks[..., :qkv_width].reshape(model_width, 3 * model_width)
         qkv_mat = spread_blocks(qkv_mat, model_width)
+        grad_mat = qkv_mat
         packed = blocks[..., qkv_width:].reshape(owners, -1)[:, :small_len].reshape(-1)
         out_mat = gather_packed(w_out.reshape(LANES, -1), core).reshape(model_width, model_width)
         up_mat = gather_packed(w_up.reshape(LANES, -1), core).reshape(model_width, FF)
         down_mat = gather_packed(w_down.reshape(LANES, -1), core).reshape(FF, model_width)
 
+        spread = one_hot_columns(jnp.arange(model_width, dtype=jnp.int32), model_width)
+
         def widen(values):
-            return values
-
-        def narrow(values):
             return values
 
         def send_sum(left, right, extra=None):
@@ -527,6 +644,7 @@
     up_bias = packed[7 * model_width : 7 * model_width + FF]
     down_bias = packed[7 * model_width + FF :]
 
+    low_inputs = inputs
     inputs = inputs.astype(jnp.float32)
     normed_one, inverse_one = layer_stats(inputs)
     act_one = round_low(normed_one * gain_one + bias_one)
@@ -562,10 +680,14 @@
         gelu_rows, slope = gate_and_slope(dot_rows(act_two, up_mat) + up_bias)
         slopes = [round_low(slope)]
         gelu_rows = round_low(gelu_rows)
-    sum_down = outer(gelu_rows, grad_rows)
-    gelu_rows, sum_down, slopes = tie((gelu_rows, sum_down, slopes))
-    sum_down = sum_down.reshape(owners, -1, model_width)
-    sum_down = lax.psum_scatter(sum_down, ALL, scatter_dimension=0, tiled=True)
+    down_parts = outer(gelu_rows, grad_rows)
+    gelu_rows, down_parts, slopes = tie((gelu_rows, down_parts, slopes))
+    down_a, down_b = [
+        lax.psum_scatter(
+            part.reshape(owners, -1, part.shape[1]), ALL, scatter_dimension=0, tiled=True
+        )
+        for part in down_parts
+    ]
 
     grad_float = grad_rows.astype(jnp.float32)
     down_bias_term = jnp.sum(grad_float, axis=0)
@@ -607,9 +729,10 @@
         grad_mixed = round_low(tail_dot(grad_mixed, head_spread))
         out_a = keep_first(mixed_a, grad_attn[:, :out_cut], out_got_a)
         out_b = keep_first(mixed_b, grad_attn[:, out_cut:], out_got_b)
-        grad_mixed, out_a, out_b = tie((grad_mixed, out_a, out_b))
-        got_a, got_b = send_half(sum_a, *order_a[1]), send_half(sum_b, *order_b[1])
-        out_got_a, out_got_b = send_half(out_a, *order_a[1]), send_half(out_b, *order_b[1])
+        rest_a = jnp.concatenate([sum_a, out_a], axis=1)
+        rest_b = jnp.concatenate([sum_b, out_b], axis=1)
+        grad_mixed, rest_a, rest_b = tie((grad_mixed, rest_a, rest_b))
+        got_a, got_b = send_half(rest_a, *order_a[1]), send_half(rest_b, *order_b[1])
     else:
         sum_out = send_sum(mixed[:, :model_width], grad_attn)
         grad_mixed = jnp.pad(grad_mixed, [(0, 0), (0, WIDE - model_width)])
@@ -618,15 +741,12 @@
     )
     grad_got = lax.ppermute(grad_other, "core", SWAP)
     if whole_rows:
-        grad_own, got_a, got_b, out_got_a, out_got_b = tie(
-            (grad_own, got_a, got_b, out_got_a, out_got_b)
-        )
-        sum_a, sum_b = add_half(sum_a, got_a), add_half(sum_b, got_b)
-        out_a, out_b = add_half(out_a, out_got_a), add_half(out_b, out_got_b)
-        rest_a = jnp.concatenate([sum_a, out_a], axis=1)
-        rest_b = jnp.concatenate([sum_b, out_b], axis=1)
+        grad_own, got_a, got_b, gelu_rows = tie((grad_own, got_a, got_b, gelu_rows))
+        rest_a, rest_b = add_half(rest_a, got_a), add_half(rest_b, got_b)
         got_a, got_b = send_half(rest_a, *order_a[2]), send_half(rest_b, *order_b[2])
+        grad_got, down_a = tie((grad_got, down_a))
     grad_qkv_rows = add_received(grad_own, grad_got)
+    rows_now = grad_qkv_rows
     if whole_rows:
         qkv_cut = (3 * WIDE // 256) * 128
         rows_a, rows_b = grad_qkv_rows[:, :qkv_cut], grad_qkv_rows[:, qkv_cut:]
@@ -634,31 +754,14 @@
         qkv_got_b = give_first(one_b, rows_b, order_b)
         qkv_a = keep_first(one_a, rows_a, qkv_got_a)
         qkv_b = keep_first(one_b, rows_b, qkv_got_b)
-        grad_qkv_rows, qkv_a, qkv_b, got_a, got_b, gelu_rows, sum_down = tie(
-            (grad_qkv_rows, qkv_a, qkv_b, got_a, got_b, gelu_rows, sum_down)
-        )
+        rows_now, qkv_a, qkv_b, got_a, got_b = tie((rows_now, qkv_a, qkv_b, got_a, got_b))
         rest = jnp.concatenate([add_half(rest_a, got_a), add_half(rest_b, got_b)], axis=1)
         qkv_got_a = send_half(qkv_a, *order_a[1])
         qkv_got_b = send_half(qkv_b, *order_b[1])
         rest_got = send_half(rest, *order_a[3])
-    grad_act_one = tail_dot(grad_qkv_rows, qkv_mat)
-    if whole_rows:
-        grad_act_one, qkv_got_a, qkv_got_b, rest_got = tie(
-            (grad_act_one, qkv_got_a, qkv_got_b, rest_got)
-        )
-        qkv_a, qkv_b = add_half(qkv_a, qkv_got_a), add_half(qkv_b, qkv_got_b)
-        qkv_got_a = send_half(qkv_a, *order_a[2])
-        qkv_got_b = send_half(qkv_b, *order_b[2])
-        rest = add_half(rest, rest_got)
-        rest_got = send_half(rest, *order_a[4])
-    grad_act_one = narrow(grad_act_one)
     qkv_sums = jnp.sum(grad_qkv_rows.astype(jnp.float32), axis=0)
-    gain_one_term = jnp.sum(grad_act_one * normed_one, axis=0)
-    bias_one_term = jnp.sum(grad_act_one, axis=0)
-    small_grad = jnp.concatenate(
+    early_small = jnp.concatenate(
         [
-            gain_one_term,
-            bias_one_term,
             qkv_sums[:model_width],
             qkv_sums[2 * WIDE : 2 * WIDE + model_width],
             bias_out_term,
@@ -668,36 +771,68 @@
             down_bias_term,
         ]
     )
-    small_grad = round_low(small_grad)
-    grad_input = grad_resid + norm_back(grad_act_one, normed_one, inverse_one, gain_one)
-    grad_input = round_low(grad_input)
-    outputs = round_low(resid + dot_rows(gelu_rows, down_mat) + down_bias)
-    if whole_rows:
-        small_rows = round_low(lead_dot(turn_a, small_grad.reshape(model_width, -1)))
-        grad_input, outputs, qkv_got_a, qkv_got_b, rest_got = tie(
-            (grad_input, outputs, qkv_got_a, qkv_got_b, rest_got)
+    grad_input, gain_one_term, bias_one_term = input_grad(
+        rows_now, grad_mat, spread, low_inputs, gain_one[None, :], grad_resid
+    )
+    if whole_rows:
+        (
+            grad_input,
+            gain_one_term,
+            bias_one_term,
+            early_small,
+            gelu_rows,
+            qkv_got_a,
+            qkv_got_b,
+            rest_got,
+        ) = tie(
+            (
+                grad_input,
+                gain_one_term,
+                bias_one_term,
+                early_small,
+                gelu_rows,
+                qkv_got_a,
+                qkv_got_b,
+                rest_got,
+            )
         )
         qkv_a, qkv_b = add_half(qkv_a, qkv_got_a), add_half(qkv_b, qkv_got_b)
+        qkv_got_a = send_half(qkv_a, *order_a[2])
+        qkv_got_b = send_half(qkv_b, *order_b[2])
+        rest = add_half(rest, rest_got)
+        rest_got = send_half(rest, *order_a[4])
+    outputs = project(gelu_rows, down_mat, resid, down_bias[None, :])
+    small_grad = jnp.concatenate([gain_one_term[0], bias_one_term[0], early_small])
+    small_grad = round_low(small_grad)
+    if whole_rows:
+        down_b, outputs, qkv_got_a, qkv_got_b, rest_got = tie(
+            (down_b, outputs, qkv_got_a, qkv_got_b, rest_got)
+        )
+    result_got = trade_out(outputs)
+    if whole_rows:
+        qkv_a, qkv_b = add_half(qkv_a, qkv_got_a), add_half(qkv_b, qkv_got_b)
         sum_qkv = jnp.concatenate([qkv_a, qkv_b], axis=1)
-        sum_qkv = halve(sum_qkv, *order_a[3])
+        sum_got = send_half(sum_qkv, *order_a[3])
         rest = add_half(rest, rest_got)
         for step in order_a[5:]:
             rest = halve(rest, *step)
-        for step in order_a[:4]:
-            small_rows = halve(small_rows, *step)
-        sum_qkv = jnp.concatenate([sum_qkv, small_rows], axis=1)
+        small_grad = small_grad.reshape(owners, small_len)
+        sum_got, result_got, small_grad = tie((sum_got, result_got, small_grad))
+        sum_qkv = add_half(sum_qkv, sum_got)
         for step in order_a[4:]:
             sum_qkv = halve(sum_qkv, *step)
+        small_parts = lax.all_to_all(small_grad, ALL, 0, 0, tiled=True)
+        grad_small = jnp.sum(small_parts.astype(jnp.float32), axis=0)
         sides = [up_cut, up_cut + out_cut, FF + out_cut]
         sum_up = jnp.concatenate([rest[:, : sides[0]], rest[:, sides[1] : sides[2]]], axis=1)
         sum_out = jnp.concatenate([rest[:, sides[0] : sides[1]], rest[:, sides[2] :]], axis=1)
         grad_qkv = pick_blocks(sum_qkv, model_width)
-        grad_small = sum_qkv[:, 3 * WIDE :]
     else:
         sum_qkv = send_sum(act_one, pick_blocks(grad_qkv_rows, model_width), small_grad)
         grad_qkv, grad_small = sum_qkv[:, :qkv_width], sum_qkv[:, qkv_width:]
-    result = trade_back(outputs)
-    grad_tokens = trade_back(grad_input)
+    result = trade_join(outputs, result_got)
+    grad_tokens = trade_join(grad_input, trade_out(grad_input))
+    sum_down = jnp.concatenate([down_a, down_b], axis=2)
     grad_small = grad_small.astype(jnp.float32).reshape(-1)[:small_len]
     grad_qkv, grad_out, grad_up, grad_down = [
         piece.astype(jnp.float32).reshape(-1) for piece in (grad_qkv, sum_out, sum_up, sum_down)

time: 589 us -> 643 us (1.092)
  waiting for transfers between devices: 180 us -> 248 us
  Pallas kernels: 58.3 us -> 87.5 us
  matrix products: 132 us -> 107 us
  other arithmetic: 74.3 us -> 58.4 us
    ppermute x32 -> x26, waiting for transfers between devices: 96.8 us -> 133 us  [swap_with(): lax.ppermute(values, axis, [(here, here ^ 1 << bit) for here in range(cou...]
    pallas_call x0 -> x2, Pallas kernels: none -> 29.5 us  [the longest x1 16 us: input_grad(): pl.pallas_call(input_grad_kernel, grid=(3 * WIDE // step,), in_specs=[pl....]
    optimization_barrier x1, waiting for transfers between devices: 21.7 us -> 48.1 us  [local(): tie((down_b, outputs, qkv_got_a, qkv_got_b, rest_got))]
    dot_general x9 -> x7, matrix products: 43.9 us -> 29 us  [tail_dot(): lax.dot_general(left_side, right_side, (((1,), (1,)), ((), ())), preferre...]
    reduce_scatter x0 -> x1, waiting for transfers between devices: none -> 13.4 us  [local(): lax.psum_scatter(part.reshape(owners, -1, part.shape[1]), ALL, scatter_di...]
    dot_general x11 -> x10, matrix products: 64 us -> 51.5 us  [dot_rows(): lax.dot_general(left, right, (((1,), (0,)), ((), ())), preferred_element_...]
    all_to_all x0 -> x1, waiting for transfers between devices: none -> 8.48 us  [local(): small_parts = lax.all_to_all(small_grad, ALL, 0, 0, tiled=True)]
    ppermute x2, waiting for transfers between devices: 10.2 us -> 1.91 us  [trade_out(): lax.ppermute(jnp.concatenate([values[span:half], values[half + span:]], a...]
  transfers between devices with their start and end apart: 41 -> 37, of which waited for: 18 -> 17; matrix products, arithmetic and copies ran while one was open for 37% -> 33% of each run, Pallas kernels for 10% -> 14%
where the time goes in v1:
time: 643 us; the launch traced here: 632 us
  waiting for transfers between devices  248 us (39%)
  matrix products  107 us (17%)
  Pallas kernels  87.5 us (14%)
  local copies, waits for them, and re-layouts  83.5 us (13%)
  other arithmetic  58.4 us (9%)
  starting transfers between devices  31.3 us (5%)
  between operations  15.5 us (2%)
    ppermute x26, waiting for transfers between devices, swap_with(): lax.ppermute(values, axis, [(here, here ^ 1 << bit) for here in range(cou...  133 us
    dot_general x10, matrix products, dot_rows(): lax.dot_general(left, right, (((1,), (0,)), ((), ())), preferred_element_...  51.5 us
    optimization_barrier x1, waiting for transfers between devices, local(): tie((down_b, outputs, qkv_got_a, qkv_got_b, rest_got))  48.1 us
    all_gather x1, waiting for transfers between devices, local(): blocks = lax.all_gather(blocks, ALL, axis=0, tiled=True)  43.4 us
    unnamed x225, local copies, waits for them, and re-layouts  33.8 us
    dot_general x7, matrix products, tail_dot(): lax.dot_general(left_side, right_side, (((1,), (1,)), ((), ())), preferre...  29 us
    pallas_call x1, Pallas kernels, attend_back(): return call(own, other, query_places, key_places, mixed, logs, grad)  27.1 us
    dot_general x12, matrix products, lead_dot(): lax.dot_general(left_side, right_side, (((0,), (0,)), ((), ())), preferre...  26.6 us
  transfers between devices with their start and end apart: 37, of which 17 were waited for; matrix products, arithmetic and copies ran while one was open for 33% of the time, Pallas kernels for 14%

profile of v1, /device:TPU:0, one launch (start us, length us, event | category | flops | bytes accessed | tf_op | source)
XLA Modules:
  0.0 631.7 jit_solution(17226171286521848515)
XLA Ops:
  53.3 20.4 %collective-permute-done.1 = bf16[68,4352]{1,0:T(8,128)(2,1)} collective-permute-done((bf16[68,4352]{1,0:T(8,128)(2,1)}, bf16[68,4352]{1,0:T(8,128)(2,1)}, u32[]{:S(2)}, u32[]{:S(2)}) %collective-permute-start.1) | collective-permute-done | bytes 591904 | tf_op jit(solution)/shard_map/ppermute | solution.py:448
  75.1 43.4 %all-gather.3.cloned.1.call-done.mat_ref = bf16[1280,4544]{1,0:T(8,128)(2,1)} async-done(((bf16[40,4544]{1,0:T(8,128)(2,1)}), bf16[1280,4544]{1,0:T(8,128)(2,1)}) %all-gather.3.cloned.1.call-update) | async-done | bytes 11632656 | tf_op jit(solution)/shard_map/all_gather | solution.py:581
  121.5 13.4 %add_convert_fusion.own_ref = bf16[512,3456]{1,0:T(8,128)(2,1)} fusion(bf16[1280,4544]{1,0:T(8,128)(2,1)} %all-gather.3.cloned.1.call-done.mat_ref, f32[3456]{0:T(1024)S(1)} %reduce.2, bf16[1088,1280]{1,0:T(8,128)(2,1)} %fusion.5.spread_ref, bf16[512,1088]{1,0:T(8,128)(2,1)S(1)} %pad_maximum_fusion.8.input_ref, f32[1088]{0:T(1024)S(1)} %get-tuple-element.243, ...), kind=kOutput, calls=%fused_computation.3 | convolution fusion | flops 5963448320 | bytes 16312320 | tf_op jit(solution)/shard_map/dot_general | solution.py:78
  149.9 9.7 %collective-permute-done.5 = bf16[136,2176]{1,0:T(8,128)(2,1)} collective-permute-done((bf16[136,2176]{1,0:T(8,128)(2,1)}, bf16[136,2176]{1,0:T(8,128)(2,1)}, u32[]{:S(2)}, u32[]{:S(2)}) %collective-permute-start.5) | collective-permute-done | bytes 591904 | tf_op jit(solution)/shard_map/ppermute | solution.py:448
  167.5 18.9 %shard_map.135 = (bf16[512,1152]{1,0:T(8,128)(2,1)S(1)}, f32[17,512]{1,0:T(8,128)S(1)}) custom-call(bf16[512,3456]{1,0:T(8,128)(2,1)} %add_convert_fusion.own_ref, bf16[512,2304]{1,0:T(8,128)(2,1)} %collective-permute-done.4.other_ref, s32[1,512]{1,0:T(1,128)S(1)} %bitcast.83, s32[1024,1]{1,0:T(8,128)S(1)} %copy.61.key_ref), custom_call_target="tpu_custom_call" | custom-call | flops 21474836480 | bytes 12582912 | tf_op jit(solution)/shard_map/pallas_call | solution.py:422
  186.4 19.3 %collective-permute-done.7 = bf16[272,2176]{1,0:T(8,128)(2,1)S(1)} collective-permute-done((bf16[272,2176]{1,0:T(8,128)(2,1)S(1)}, bf16[272,2176]{1,0:T(8,128)(2,1)S(1)}, u32[]{:S(2)}, u32[]{:S(2)}) %collective-permute-start.7) | collective-permute-done | bytes 1183776 | tf_op jit(solution)/shard_map/ppermute | solution.py:448
  211.3 7.5 %fusion.96 = (f32[512]{0:T(512)}, f32[512,1088]{1,0:T(8,128)S(1)}) fusion(f32[1088]{0:T(1024)} %get-tuple-element.240, bf16[1280,4544]{1,0:T(8,128)(2,1)} %all-gather.3.cloned.1.call-done.mat_ref, bf16[512,1152]{1,0:T(8,128)(2,1)} %copy-done.15, bf16[1152,1280]{1,0:T(8,128)(2,1)} %fusion.4, bf16[512,1088]{1,0:T(8,128)(2,1)S(1)} %pad_maximum_fusion.8.input_ref), kind=kOutput, calls=%fused_computation.240 | convolution fusion | flops 2938895872 | bytes 10430464 | tf_op jit(solution)/shard_map/dot_general | solution.py:78
  237.2 7.1 %add_convert_fusion.3 = (bf16[512,2176]{1,0:T(8,128)(2,1)}, bf16[512,2176]{1,0:T(8,128)(2,1)S(1)}) fusion(f32[2176]{0:T(1024)S(1)} %copy-done.71, bf16[512,1088]{0,1:T(8,128)(2,1)S(1)} %convolution_convert_fusion.12, bf16[1088,2176]{1,0:T(8,128)(2,1)S(1)} %constant_dynamic-update-slice_fusion.4), kind=kOutput, calls=%fused_computation.33 | convolution fusion | flops 2446589952 | bytes 10314240 | tf_op jit(solution)/shard_map/dot_general | solution.py:78
  244.3 6.9 %add_convert_fusion.4 = (bf16[512,2176]{1,0:T(8,128)(2,1)}, bf16[512,2176]{1,0:T(8,128)(2,1)S(1)}) fusion(f32[2176]{0:T(1024)S(1)} %copy-done.70, bf16[512,1088]{0,1:T(8,128)(2,1)S(1)} %convolution_convert_fusion.13, bf16[1088,2176]{1,0:T(8,128)(2,1)S(1)} %constant_dynamic-update-slice_fusion.1), kind=kOutput, calls=%fused_computation.34 | convolution fusion | flops 2446589952 | bytes 10314240 | tf_op jit(solution)/shard_map/dot_general | solution.py:78
  252.5 9.6 %shard_map.136 = (bf16[4352,512]{1,0:T(8,128)(2,1)S(1)}, bf16[4352,576]{1,0:T(8,128)(2,1)S(1)}) custom-call(bf16[512,4352]{1,0:T(8,128)(2,1)S(1)} %pad_maximum_fusion.left_ref, bf16[512,1088]{1,0:T(8,128)(2,1)S(1)} %copy-done.7), custom_call_target="tpu_custom_call" | custom-call | flops 4848615424 | bytes 16777216 | tf_op jit(solution)/shard_map/pallas_call | solution.py:287
  266.6 7.0 %convert_reduce_fusion.2 = (bf16[2176]{0:T(1024)(128)(2,1)}, bf16[512,2176]{1,0:T(8,128)(2,1)S(1)}) fusion(bf16[512,2176]{1,0:T(8,128)(2,1)} %get-tuple-element.108, bf16[512,1088]{1,0:T(8,128)(2,1)S(1)} %copy-done.7, bf16[4352,1088]{1,0:T(8,128)(2,1)} %all-gather.5.cloned.1.call-done.mat_ref), kind=kOutput, calls=%fused_computation.32 | convolution fusion | flops 2429876224 | bytes 10588416 | tf_op jit(solution)/shard_map/dot_general | solution.py:39
  318.8 6.9 %convolution_convert_fusion.10.grad_ref = bf16[512,1152]{1,0:T(8,128)(2,1)S(1)} fusion(bf16[1152,1280]{1,0:T(8,128)(2,1)} %fusion.4, bf16[512,1088]{1,0:T(8,128)(2,1)} %copy-done.54, bf16[1280,4544]{1,0:T(8,128)(2,1)} %all-gather.3.cloned.1.call-done.mat_ref), kind=kOutput, calls=%fused_computation.56 | convolution fusion | flops 2937257984 | bytes 8257536 | tf_op jit(solution)/shard_map/dot_general | solution.py:39
  332.9 27.1 %shard_map.137 = (bf16[512,3456]{1,0:T(8,128)(2,1)}, bf16[512,2304]{1,0:T(8,128)(2,1)}) custom-call(bf16[512,3456]{1,0:T(8,128)(2,1)} %add_convert_fusion.own_ref, bf16[512,2304]{1,0:T(8,128)(2,1)} %collective-permute-done.4.other_ref, s32[1,512]{1,0:T(1,128)S(1)} %bitcast.84, s32[1024,1]{1,0:T(8,128)S(1)} %copy-done.13, bf16[512,1152]{1,0:T(8,128)(2,1)S(1)} %copy-done.18, ...), custom_call_target="tpu_custom_call" | custom-call | flops 32212254720 | bytes 12582912 | tf_op jit(solution)/shard_map/pallas_call | solution.py:431
  364.5 40.5 %collective-permute-done.15 = bf16[272,2688]{1,0:T(8,128)(2,1)} collective-permute-done((bf16[272,2688]{1,0:T(8,128)(2,1)}, bf16[272,2688]{1,0:T(8,128)(2,1)}, u32[]{:S(2)}, u32[]{:S(2)}) %collective-permute-start.15) | collective-permute-done | bytes 1462304 | tf_op jit(solution)/shard_map/ppermute | solution.py:448
  405.1 9.9 %collective-permute-done.16 = bf16[272,2752]{1,0:T(8,128)(2,1)} collective-permute-done((bf16[272,2752]{1,0:T(8,128)(2,1)}, bf16[272,2752]{1,0:T(8,128)(2,1)}, u32[]{:S(2)}, u32[]{:S(2)}) %collective-permute-start.16) | collective-permute-done | bytes 1497120 | tf_op jit(solution)/shard_map/ppermute | solution.py:448
  415.0 13.4 %reduce-scatter.6.cloned.1.call-done = bf16[1,136,512]{2,1,0:T(8,128)(2,1)} async-done(((bf16[32,136,512]{2,1,0:T(8,128)(2,1)}), bf16[1,136,512]{2,1,0:T(8,128)(2,1)}) %reduce-scatter.6.cloned.1.call-update) | async-done | bytes 139280 | tf_op jit(solution)/shard_map/reduce_scatter | solution.py:686
  443.5 6.2 concatenate.122
  455.4 12.0 %collective-permute-done.20 = bf16[136,2688]{1,0:T(8,128)(2,1)} collective-permute-done((bf16[136,2688]{1,0:T(8,128)(2,1)}, bf16[136,2688]{1,0:T(8,128)(2,1)}, u32[]{:S(2)}, u32[]{:S(2)}) %collective-permute-start.20) | collective-permute-done | bytes 731168 | tf_op jit(solution)/shard_map/ppermute | solution.py:448
  473.8 16.0 %shard_map.139 = (bf16[512,1088]{1,0:T(8,128)(2,1)S(1)}, f32[1,1088]{1,0:T(1,128)S(1)}, f32[1,1088]{1,0:T(1,128)S(1)}) custom-call(bf16[512,3456]{1,0:T(8,128)(2,1)} %copy-done.1, bf16[1280,4544]{1,0:T(8,128)(2,1)} %all-gather.3.cloned.1.call-done.mat_ref, bf16[1088,1280]{1,0:T(8,128)(2,1)} %fusion.5.spread_ref, bf16[512,1088]{1,0:T(8,128)(2,1)S(1)} %copy-done.3, ...), custom_call_target="tpu_custom_call" | custom-call | flops 15032385536 | bytes 20971520 | tf_op jit(solution)/shard_map/pallas_call | solution.py:350
  495.3 8.3 %collective-permute-done.23 = bf16[272,1792]{1,0:T(8,128)(2,1)S(1)} collective-permute-done((bf16[272,1792]{1,0:T(8,128)(2,1)S(1)}, bf16[272,1792]{1,0:T(8,128)(2,1)S(1)}, u32[]{:S(2)}, u32[]{:S(2)}) %collective-permute-start.23) | collective-permute-done | bytes 974880 | tf_op jit(solution)/shard_map/ppermute | solution.py:448
  524.1 13.4 %shard_map.140 = bf16[512,1088]{1,0:T(8,128)(2,1)S(1)} custom-call(bf16[512,4352]{1,0:T(8,128)(2,1)S(1)} %copy-done.9, bf16[4352,1088]{1,0:T(8,128)(2,1)S(1)} %copy-done.14, f32[512,1088]{1,0:T(8,128)S(1)} %copy-done.5, f32[1,1088]{1,0:T(1,128)S(1)} %broadcast_in_dim.25.bias_ref), custom_call_target="tpu_custom_call" | custom-call | flops 15032385536 | bytes 20971520 | tf_op jit(solution)/shard_map/pallas_call | solution.py:398
  537.6 48.1 %reduce-scatter.8.cloned.1.call-done = bf16[1,136,576]{2,1,0:T(8,128)(2,1)} async-done(((bf16[32,136,576]{2,1,0:T(8,128)(2,1)}), bf16[1,136,576]{2,1,0:T(8,128)(2,1)}) %reduce-scatter.8.cloned.1.call-update) | async-done | bytes 156688 | tf_op jit(solution)/shard_map/optimization_barrier | solution.py:808
  606.7 5.8 all-to-all-start
  614.3 8.5 %all-to-all-done = bf16[32,2,204]{2,1,0:T(2,128)(2,1)S(1)} async-done(((bf16[32,2,204]{2,1,0:T(2,128)(2,1)}), bf16[32,2,204]{2,1,0:T(2,128)(2,1)S(1)}, u32[]{:S(2)}, u32[]{:S(2)}) %all-to-all-start) | async-done | bytes 26144 | tf_op jit(solution)/shard_map/all_to_all | solution.py:824
  (443 shorter events, 236.8 us)
Async XLA Ops:
  7.2 111.3 %all-gather.3.cloned.1.call-start = ((), (), s32[]{:S(2)}) async-start(), calls=%async_computation.3 | async-start | bytes 12165120 | tf_op jit(solution)/shard_map/all_gather | solution.py:581
  11.2 255.3 %all-gather.5.cloned.1.call-start = ((), (), s32[]{:S(2)}) async-start(), calls=%async_computation.4 | async-start | bytes 10340352 | tf_op jit(solution)/shard_map/all_gather | solution.py:582
  11.7 30.0 %collective-permute-start = (bf16[34,4352]{1,0:T(8,128)(2,1)S(1)}, bf16[34,4352]{1,0:T(8,128)(2,1)S(1)}, u32[]{:S(2)}, u32[]{:S(2)}) collective-permute-start(bf16[34,4352]{1,0:T(8,128)(2,1)S(1)} %reshape.198), channel_id=1, source_target_pairs={{0,16},{4,20},{8,24},{12,28},{16,0},{20,4},{24,8},{28,12},{1,17},{... | collective-permute-start | bytes 887816 | tf_op jit(solution)/shard_map/ppermute | solution.py:448
  16.6 27.6 %collective-permute-start.2 = (bf16[256,1088]{0,1:T(8,128)(2,1)}, bf16[256,1088]{0,1:T(8,128)(2,1)}, u32[]{:S(2)}, u32[]{:S(2)}) collective-permute-start(bf16[256,1088]{0,1:T(8,128)(2,1)} %dynamic-slice_bitcast_fusion.1), channel_id=1, source_target_pairs={{0,2},{2,0},{1,3},{3,1},{4,6},{6,4},{5,7},{7,5},{8,10},{10,8},{9,1... | collective-permute-start | bytes 1671176 | tf_op jit(solution)/shard_map/ppermute | solution.py:525
  20.0 25.6 %collective-permute-start.3 = (bf16[256,1088]{0,1:T(8,128)(2,1)}, bf16[256,1088]{0,1:T(8,128)(2,1)}, u32[]{:S(2)}, u32[]{:S(2)}) collective-permute-start(bf16[256,1088]{0,1:T(8,128)(2,1)} %dynamic-slice_bitcast_fusion), channel_id=1, source_target_pairs={{0,2},{2,0},{1,3},{3,1},{4,6},{6,4},{5,7},{7,5},{8,10},{10,8},{9,1... | collective-permute-start | bytes 1671176 | tf_op jit(solution)/shard_map/ppermute | solution.py:525
  21.5 406.9 %reduce-scatter.6.cloned.1.call-start = ((), (), s32[]{:S(2)}) async-start(), calls=%async_computation.5 | async-start | bytes 4595712 | tf_op jit(solution)/shard_map/reduce_scatter | solution.py:686
  42.6 31.1 %collective-permute-start.1 = (bf16[68,4352]{1,0:T(8,128)(2,1)}, bf16[68,4352]{1,0:T(8,128)(2,1)}, u32[]{:S(2)}, u32[]{:S(2)}) collective-permute-start(bf16[68,4352]{1,0:T(8,128)(2,1)} %pad_maximum_fusion.13), channel_id=1, source_target_pairs={{0,8},{4,12},{8,0},{12,4},{16,24},{20,28},{24,16},{28,20},{1,9},{5... | collective-permute-start | bytes 1775624 | tf_op jit(solution)/shard_map/ppermute | solution.py:448
  138.1 29.3 %collective-permute-start.4 = (bf16[512,2304]{1,0:T(8,128)(2,1)}, bf16[512,2304]{1,0:T(8,128)(2,1)}, u32[]{:S(2)}, u32[]{:S(2)}) collective-permute-start(bf16[512,2304]{1,0:T(8,128)(2,1)} %slice.456), channel_id=1, source_target_pairs={{0,1},{1,0},{2,3},{3,2},{4,5},{5,4},{6,7},{7,6},{8,9},{9,8},{10,11... | collective-permute-start | bytes 7077896 | tf_op jit(solution)/shard_map/ppermute | solution.py:654
  140.8 23.2 %collective-permute-start.6 = (bf16[136,2176]{1,0:T(8,128)(2,1)S(1)}, bf16[136,2176]{1,0:T(8,128)(2,1)S(1)}, u32[]{:S(2)}, u32[]{:S(2)}) collective-permute-start(bf16[136,2176]{1,0:T(8,128)(2,1)S(1)} %get-tuple-element.206), channel_id=1, source_target_pairs={{0,4},{4,0},{8,12},{12,8},{16,20},{20,16},{24,28},{28,24},{1,5},{5... | collective-permute-start | bytes 1775624 | tf_op jit(solution)/shard_map/ppermute | solution.py:448
  165.3 40.4 %collective-permute-start.7 = (bf16[272,2176]{1,0:T(8,128)(2,1)S(1)}, bf16[272,2176]{1,0:T(8,128)(2,1)S(1)}, u32[]{:S(2)}, u32[]{:S(2)}) collective-permute-start(bf16[272,2176]{1,0:T(8,128)(2,1)S(1)} %pad_maximum_fusion.6), channel_id=1, source_target_pairs={{0,4},{4,0},{8,12},{12,8},{16,20},{20,16},{24,28},{28,24},{1,5},{5... | collective-permute-start | bytes 3551240 | tf_op jit(solution)/shard_map/ppermute | solution.py:448
  166.3 41.2 %collective-permute-start.8 = (bf16[272,2176]{1,0:T(8,128)(2,1)S(1)}, bf16[272,2176]{1,0:T(8,128)(2,1)S(1)}, u32[]{:S(2)}, u32[]{:S(2)}) collective-permute-start(bf16[272,2176]{1,0:T(8,128)(2,1)S(1)} %pad_maximum_fusion.7), channel_id=1, source_target_pairs={{0,2},{2,0},{1,3},{3,1},{4,6},{6,4},{5,7},{7,5},{8,10},{10,8},{9,1... | collective-permute-start | bytes 3551240 | tf_op jit(solution)/shard_map/ppermute | solution.py:448
  276.6 23.1 %collective-permute-start.11 = (bf16[544,2176]{1,0:T(8,128)(2,1)}, bf16[544,2176]{1,0:T(8,128)(2,1)}, u32[]{:S(2)}, u32[]{:S(2)}) collective-permute-start(bf16[544,2176]{1,0:T(8,128)(2,1)} %convolution_convert_fusion.3), channel_id=1, source_target_pairs={{0,1},{1,0},{2,3},{3,2},{4,5},{5,4},{6,7},{7,6},{8,9},{9,8},{10,11... | collective-permute-start | bytes 7102472 | tf_op jit(solution)/shard_map/ppermute | solution.py:448
  288.1 297.6 %reduce-scatter.8.cloned.1.call-start = ((), (), s32[]{:S(2)}) async-start(), calls=%async_computation.6 | async-start | bytes 5744640
  360.0 55.0 %collective-permute-start.17 = (bf16[512,2304]{1,0:T(8,128)(2,1)}, bf16[512,2304]{1,0:T(8,128)(2,1)}, u32[]{:S(2)}, u32[]{:S(2)}) collective-permute-start(bf16[512,2304]{1,0:T(8,128)(2,1)} %get-tuple-element.126), channel_id=1, source_target_pairs={{0,1},{1,0},{2,3},{3,2},{4,5},{5,4},{6,7},{7,6},{8,9},{9,8},{10,11... | collective-permute-start | bytes 7077896 | tf_op jit(solution)/shard_map/ppermute | solution.py:742
  361.3 53.6 %collective-permute-start.16 = (bf16[272,2752]{1,0:T(8,128)(2,1)}, bf16[272,2752]{1,0:T(8,128)(2,1)}, u32[]{:S(2)}, u32[]{:S(2)}) collective-permute-start(bf16[272,2752]{1,0:T(8,128)(2,1)} %slice.394), channel_id=1, source_target_pairs={{0,2},{2,0},{1,3},{3,1},{4,6},{6,4},{5,7},{7,5},{8,10},{10,8},{9,1... | collective-permute-start | bytes 4491272 | tf_op jit(solution)/shard_map/ppermute | solution.py:448
  364.5 40.6 %collective-permute-start.15 = (bf16[272,2688]{1,0:T(8,128)(2,1)}, bf16[272,2688]{1,0:T(8,128)(2,1)}, u32[]{:S(2)}, u32[]{:S(2)}) collective-permute-start(bf16[272,2688]{1,0:T(8,128)(2,1)} %slice.393), channel_id=1, source_target_pairs={{0,4},{4,0},{8,12},{12,8},{16,20},{20,16},{24,28},{28,24},{1,5},{5... | collective-permute-start | bytes 4386824 | tf_op jit(solution)/shard_map/ppermute | solution.py:448
  439.3 28.1 %collective-permute-start.20 = (bf16[136,2688]{1,0:T(8,128)(2,1)}, bf16[136,2688]{1,0:T(8,128)(2,1)}, u32[]{:S(2)}, u32[]{:S(2)}) collective-permute-start(bf16[136,2688]{1,0:T(8,128)(2,1)} %slice.476), channel_id=1, source_target_pairs={{0,2},{2,0},{1,3},{3,1},{4,6},{6,4},{5,7},{7,5},{8,10},{10,8},{9,1... | collective-permute-start | bytes 2193416 | tf_op jit(solution)/shard_map/ppermute | solution.py:448
  442.2 25.3 %collective-permute-start.21 = (bf16[136,2752]{1,0:T(8,128)(2,1)}, bf16[136,2752]{1,0:T(8,128)(2,1)}, u32[]{:S(2)}, u32[]{:S(2)}) collective-permute-start(bf16[136,2752]{1,0:T(8,128)(2,1)} %slice.477), channel_id=1, source_target_pairs={{0,4},{4,0},{8,12},{12,8},{16,20},{20,16},{24,28},{28,24},{1,5},{5... | collective-permute-start | bytes 2245640 | tf_op jit(solution)/shard_map/ppermute | solution.py:448
  467.5 27.8 %collective-permute-start.22 = (bf16[272,1664]{1,0:T(8,128)(2,1)S(1)}, bf16[272,1664]{1,0:T(8,128)(2,1)}, u32[]{:S(2)}, u32[]{:S(2)}) collective-permute-start(bf16[272,1664]{1,0:T(8,128)(2,1)S(1)} %slice.407), channel_id=1, source_target_pairs={{0,4},{4,0},{8,12},{12,8},{16,20},{20,16},{24,28},{28,24},{1,5},{5... | collective-permute-start | bytes 2715656 | tf_op jit(solution)/shard_map/ppermute | solution.py:448
  467.7 35.9 %collective-permute-start.23 = (bf16[272,1792]{1,0:T(8,128)(2,1)S(1)}, bf16[272,1792]{1,0:T(8,128)(2,1)S(1)}, u32[]{:S(2)}, u32[]{:S(2)}) collective-permute-start(bf16[272,1792]{1,0:T(8,128)(2,1)S(1)} %slice.408), channel_id=1, source_target_pairs={{0,2},{2,0},{1,3},{3,1},{4,6},{6,4},{5,7},{7,5},{8,10},{10,8},{9,1... | collective-permute-start | bytes 2924552 | tf_op jit(solution)/shard_map/ppermute | solution.py:448
  506.1 79.6 %collective-permute-start.25 = (bf16[136,1664]{1,0:T(8,128)(2,1)}, bf16[136,1664]{1,0:T(8,128)(2,1)}, u32[]{:S(2)}, u32[]{:S(2)}) collective-permute-start(bf16[136,1664]{1,0:T(8,128)(2,1)} %slice.485), channel_id=1, source_target_pairs={{0,2},{2,0},{1,3},{3,1},{4,6},{6,4},{5,7},{7,5},{8,10},{10,8},{9,1... | collective-permute-start | bytes 1357832 | tf_op jit(solution)/shard_map/ppermute | solution.py:448
  508.4 77.3 %collective-permute-start.26 = (bf16[136,1792]{1,0:T(8,128)(2,1)}, bf16[136,1792]{1,0:T(8,128)(2,1)}, u32[]{:S(2)}, u32[]{:S(2)}) collective-permute-start(bf16[136,1792]{1,0:T(8,128)(2,1)} %slice.486), channel_id=1, source_target_pairs={{0,4},{4,0},{8,12},{12,8},{16,20},{20,16},{24,28},{28,24},{1,5},{5... | collective-permute-start | bytes 1462280 | tf_op jit(solution)/shard_map/ppermute | solution.py:448
  515.0 70.6 %collective-permute-start.27 = (bf16[34,5440]{1,0:T(8,128)(2,1)}, bf16[34,5440]{1,0:T(8,128)(2,1)}, u32[]{:S(2)}, u32[]{:S(2)}) collective-permute-start(bf16[34,5440]{1,0:T(8,128)(2,1)} %slice.487), channel_id=1, source_target_pairs={{0,16},{4,20},{8,24},{12,28},{16,0},{20,4},{24,8},{28,12},{1,17},{... | collective-permute-start | bytes 1109768 | tf_op jit(solution)/shard_map/ppermute | solution.py:448
  518.0 78.2 %collective-permute-start.30 = (bf16[256,1088]{0,1:T(8,128)(2,1)}, bf16[256,1088]{0,1:T(8,128)(2,1)}, u32[]{:S(2)}, u32[]{:S(2)}) collective-permute-start(bf16[256,1088]{0,1:T(8,128)(2,1)} %copy.69), channel_id=1, source_target_pairs={{0,2},{2,0},{1,3},{3,1},{4,6},{6,4},{5,7},{7,5},{8,10},{10,8},{9,1... | collective-permute-start | bytes 1671176 | tf_op jit(solution)/shard_map/ppermute | solution.py:529
  (116 other events, 1200.5 us)
Sparse Core Ops, SparseCore 0:
  11.5 106.9 all-gather.2
  121.3 101.1 all-gather.4
  288.2 140.1 reduce-scatter.5
  430.7 154.9 reduce-scatter.7

commit v2 on v1

--- a/solution.py
+++ b/solution.py
@@ -471,6 +471,26 @@
     return round_low(kept.astype(jnp.float32) + got.astype(jnp.float32))
 
 
+def pick_half(values, axis, bit, other):
+    here = (lax.axis_index(axis) >> bit) & 1
+    return lax.dynamic_index_in_dim(values, here ^ other, 1, keepdims=False)
+
+
+def pair_up(values, low):
+    lead, rest = values.shape[0], values.shape[1:]
+    return values.reshape((lead // (2 * low), 2, low) + rest)
+
+
+def send_block(values, axis, bit, low):
+    return swap_with(pick_half(pair_up(values, low), axis, bit, 1), axis, bit)
+
+
+def add_block(values, got, axis, bit, low):
+    kept = pick_half(pair_up(values, low), axis, bit, 0)
+    total = round_low(kept.astype(jnp.float32) + got.astype(jnp.float32))
+    return total.reshape((-1,) + values.shape[1:])
+
+
 def double(values, axis, bit):
     return jnp.concatenate([values, swap_with(values, axis, bit)], axis=0)
 
@@ -682,12 +702,15 @@
         gelu_rows = round_low(gelu_rows)
     down_parts = outer(gelu_rows, grad_rows)
     gelu_rows, down_parts, slopes = tie((gelu_rows, down_parts, slopes))
-    down_a, down_b = [
-        lax.psum_scatter(
-            part.reshape(owners, -1, part.shape[1]), ALL, scatter_dimension=0, tiled=True
-        )
-        for part in down_parts
-    ]
+    down_a, down_b = [part.reshape(owners, -1, part.shape[1]) for part in down_parts]
+    if whole_rows:
+        down_got_a = send_block(down_a, "core", 0, 1)
+        down_got_b = send_block(down_b, "core", 0, 1)
+    else:
+        down_a, down_b = [
+            lax.psum_scatter(part, ALL, scatter_dimension=0, tiled=True)
+            for part in (down_a, down_b)
+        ]
 
     grad_float = grad_rows.astype(jnp.float32)
     down_bias_term = jnp.sum(grad_float, axis=0)
@@ -707,7 +730,13 @@
         got_a = give_first(two_a, pre_a, order_a)
         got_b = give_first(two_b, pre_b, order_b)
         back_a, back_b = tail_dot(pre_a, up_a), tail_dot(pre_b, up_b)
-        back_a, back_b, got_a, got_b = tie((back_a, back_b, got_a, got_b))
+        back_a, back_b, got_a, got_b, down_got_a, down_got_b = tie(
+            (back_a, back_b, got_a, got_b, down_got_a, down_got_b)
+        )
+        down_a = add_block(down_a, down_got_a, "core", 0, 1)
+        down_b = add_block(down_b, down_got_b, "core", 0, 1)
+        down_got_a = send_block(down_a, *order_a[1], 2)
+        down_got_b = send_block(down_b, *order_b[1], 1)
         sum_a = keep_first(two_a, pre_a, got_a)
         sum_b = keep_first(two_b, pre_b, got_b)
         back_a, back_b, sum_a, sum_b = tie((back_a, back_b, sum_a, sum_b))
@@ -731,7 +760,13 @@
         out_b = keep_first(mixed_b, grad_attn[:, out_cut:], out_got_b)
         rest_a = jnp.concatenate([sum_a, out_a], axis=1)
         rest_b = jnp.concatenate([sum_b, out_b], axis=1)
-        grad_mixed, rest_a, rest_b = tie((grad_mixed, rest_a, rest_b))
+        grad_mixed, rest_a, rest_b, down_got_a, down_got_b = tie(
+            (grad_mixed, rest_a, rest_b, down_got_a, down_got_b)
+        )
+        down_a = add_block(down_a, down_got_a, *order_a[1], 2)
+        down_b = add_block(down_b, down_got_b, *order_b[1], 1)
+        down_got_a = send_block(down_a, *order_a[2], 1)
+        down_got_b = send_block(down_b, *order_b[2], 1)
         got_a, got_b = send_half(rest_a, *order_a[1]), send_half(rest_b, *order_b[1])
     else:
         sum_out = send_sum(mixed[:, :model_width], grad_attn)
@@ -741,10 +776,18 @@
     )
     grad_got = lax.ppermute(grad_other, "core", SWAP)
     if whole_rows:
-        grad_own, got_a, got_b, gelu_rows = tie((grad_own, got_a, got_b, gelu_rows))
+        grad_own, got_a, got_b, gelu_rows, down_got_a, down_got_b = tie(
+            (grad_own, got_a, got_b, gelu_rows, down_got_a, down_got_b)
+        )
         rest_a, rest_b = add_half(rest_a, got_a), add_half(rest_b, got_b)
         got_a, got_b = send_half(rest_a, *order_a[2]), send_half(rest_b, *order_b[2])
-        grad_got, down_a = tie((grad_got, down_a))
+        down_a = add_block(down_a, down_got_a, *order_a[2], 1)
+        down_b = add_block(down_b, down_got_b, *order_b[2], 1)
+        sum_down = jnp.concatenate([down_a, down_b], axis=2)
+        down_got = send_block(sum_down, *order_a[3], 1)
+    outputs = project(gelu_rows, down_mat, resid, down_bias[None, :])
+    if whole_rows:
+        grad_got, outputs = tie((grad_got, outputs))
     grad_qkv_rows = add_received(grad_own, grad_got)
     rows_now = grad_qkv_rows
     if whole_rows:
@@ -754,7 +797,10 @@
         qkv_got_b = give_first(one_b, rows_b, order_b)
         qkv_a = keep_first(one_a, rows_a, qkv_got_a)
         qkv_b = keep_first(one_b, rows_b, qkv_got_b)
-        rows_now, qkv_a, qkv_b, got_a, got_b = tie((rows_now, qkv_a, qkv_b, got_a, got_b))
+        rows_now, qkv_a, qkv_b, got_a, got_b, down_got = tie(
+            (rows_now, qkv_a, qkv_b, got_a, got_b, down_got)
+        )
+        sum_down = add_block(sum_down, down_got, *order_a[3], 1)
         rest = jnp.concatenate([add_half(rest_a, got_a), add_half(rest_b, got_b)], axis=1)
         qkv_got_a = send_half(qkv_a, *order_a[1])
         qkv_got_b = send_half(qkv_b, *order_b[1])
@@ -780,7 +826,6 @@
             gain_one_term,
             bias_one_term,
             early_small,
-            gelu_rows,
             qkv_got_a,
             qkv_got_b,
             rest_got,
@@ -790,7 +835,6 @@
                 gain_one_term,
                 bias_one_term,
                 early_small,
-                gelu_rows,
                 qkv_got_a,
                 qkv_got_b,
                 rest_got,
@@ -801,12 +845,13 @@
         qkv_got_b = send_half(qkv_b, *order_b[2])
         rest = add_half(rest, rest_got)
         rest_got = send_half(rest, *order_a[4])
-    outputs = project(gelu_rows, down_mat, resid, down_bias[None, :])
+        for step in order_a[4:]:
+            sum_down = add_block(sum_down, send_block(sum_down, *step, 1), *step, 1)
     small_grad = jnp.concatenate([gain_one_term[0], bias_one_term[0], early_small])
     small_grad = round_low(small_grad)
     if whole_rows:
-        down_b, outputs, qkv_got_a, qkv_got_b, rest_got = tie(
-            (down_b, outputs, qkv_got_a, qkv_got_b, rest_got)
+        outputs, sum_down, qkv_got_a, qkv_got_b, rest_got = tie(
+            (outputs, sum_down, qkv_got_a, qkv_got_b, rest_got)
         )
     result_got = trade_out(outputs)
     if whole_rows:
@@ -832,7 +877,8 @@
         grad_qkv, grad_small = sum_qkv[:, :qkv_width], sum_qkv[:, qkv_width:]
     result = trade_join(outputs, result_got)
     grad_tokens = trade_join(grad_input, trade_out(grad_input))
-    sum_down = jnp.concatenate([down_a, down_b], axis=2)
+    if not whole_rows:
+        sum_down = jnp.concatenate([down_a, down_b], axis=2)
     grad_small = grad_small.astype(jnp.float32).reshape(-1)[:small_len]
     grad_qkv, grad_out, grad_up, grad_down = [
         piece.astype(jnp.float32).reshape(-1) for piece in (grad_qkv, sum_out, sum_up, sum_down)

time: 643 us -> 580 us (0.902)
  waiting for transfers between devices: 248 us -> 173 us
  starting transfers between devices: 31.3 us -> 40.7 us
    optimization_barrier x1 -> x0, waiting for transfers between devices: 48.1 us -> none  [local(): tie((down_b, outputs, qkv_got_a, qkv_got_b, rest_got))]
    reduce_scatter x1 -> x0, waiting for transfers between devices: 13.4 us -> none  [local(): lax.psum_scatter(part.reshape(owners, -1, part.shape[1]), ALL, scatter_di...]
    ppermute x26 -> x34, waiting for transfers between devices: 133 us -> 123 us  [swap_with(): lax.ppermute(values, axis, [(here, here ^ 1 << bit) for here in range(cou...]
    ppermute x26 -> x34, starting transfers between devices: 22.6 us -> 32.1 us  [swap_with(): lax.ppermute(values, axis, [(here, here ^ 1 << bit) for here in range(cou...]
    dot_general x7, matrix products: 29 us -> 38 us  [tail_dot(): lax.dot_general(left_side, right_side, (((1,), (1,)), ((), ())), preferre...]
    all_to_all x1, waiting for transfers between devices: 8.48 us -> 1.35 us  [local(): small_parts = lax.all_to_all(small_grad, ALL, 0, 0, tiled=True)]
    unnamed x225 -> x253, local copies, waits for them, and re-layouts: 33.8 us -> 29.5 us
    convert_element_type x14 -> x21, other arithmetic: 20.8 us -> 25 us  [round_low(): return values.astype(jnp.bfloat16)]
  transfers between devices with their start and end apart: 37 -> 43, of which waited for: 17 -> 18; matrix products, arithmetic and copies ran while one was open for 33% -> 35% of each run, Pallas kernels for 14% -> 15%
where the time goes in v2:
time: 580 us; the launch traced here: 569 us
  waiting for transfers between devices  173 us (30%)
  matrix products  109 us (19%)
  Pallas kernels  85.7 us (15%)
  local copies, waits for them, and re-layouts  81.3 us (14%)
  other arithmetic  63.8 us (11%)
  starting transfers between devices  40.7 us (7%)
  between operations  15.8 us (3%)
    ppermute x34, waiting for transfers between devices, swap_with(): lax.ppermute(values, axis, [(here, here ^ 1 << bit) for here in range(cou...  123 us
    dot_general x10, matrix products, dot_rows(): lax.dot_general(left, right, (((1,), (0,)), ((), ())), preferred_element_...  49.6 us
    all_gather x1, waiting for transfers between devices, local(): blocks = lax.all_gather(blocks, ALL, axis=0, tiled=True)  43.6 us
    dot_general x7, matrix products, tail_dot(): lax.dot_general(left_side, right_side, (((1,), (1,)), ((), ())), preferre...  38 us
    ppermute x34, starting transfers between devices, swap_with(): lax.ppermute(values, axis, [(here, here ^ 1 << bit) for here in range(cou...  32.1 us
    unnamed x253, local copies, waits for them, and re-layouts  29.5 us
    pallas_call x1, Pallas kernels, attend_back(): return call(own, other, query_places, key_places, mixed, logs, grad)  26.7 us
    convert_element_type x21, other arithmetic, round_low(): return values.astype(jnp.bfloat16)  25 us
  transfers between devices with their start and end apart: 43, of which 18 were waited for; matrix products, arithmetic and copies ran while one was open for 35% of the time, Pallas kernels for 15%

profile of v2, /device:TPU:0, one launch (start us, length us, event | category | flops | bytes accessed | tf_op | source)
XLA Modules:
  0.0 569.4 jit_solution(522556295673991141)
XLA Ops:
  50.3 22.6 %collective-permute-done.1 = bf16[68,4352]{1,0:T(8,128)(2,1)} collective-permute-done((bf16[68,4352]{1,0:T(8,128)(2,1)}, bf16[68,4352]{1,0:T(8,128)(2,1)}, u32[]{:S(2)}, u32[]{:S(2)}) %collective-permute-start.1) | collective-permute-done | bytes 591904 | tf_op jit(solution)/shard_map/ppermute | solution.py:448
  74.2 43.6 %all-gather.3.cloned.1.call-done.mat_ref = bf16[1280,4544]{1,0:T(8,128)(2,1)} async-done(((bf16[40,4544]{1,0:T(8,128)(2,1)}), bf16[1280,4544]{1,0:T(8,128)(2,1)}) %all-gather.3.cloned.1.call-update) | async-done | bytes 11632656 | tf_op jit(solution)/shard_map/all_gather | solution.py:601
  121.0 13.0 %add_convert_fusion.own_ref = bf16[512,3456]{1,0:T(8,128)(2,1)} fusion(bf16[1280,4544]{1,0:T(8,128)(2,1)} %all-gather.3.cloned.1.call-done.mat_ref, f32[3456]{0:T(1024)S(1)} %reduce.2, bf16[1088,1280]{1,0:T(8,128)(2,1)} %fusion.6.spread_ref, bf16[512,1088]{1,0:T(8,128)(2,1)S(1)} %pad_maximum_fusion.8.input_ref, f32[1088]{0:T(1024)S(1)} %get-tuple-element.255, ...), kind=kOutput, calls=%fused_computation.3 | convolution fusion | flops 5963448320 | bytes 16312320 | tf_op jit(solution)/shard_map/dot_general | solution.py:78
  144.8 11.7 %collective-permute-done.6 = bf16[136,2176]{1,0:T(8,128)(2,1)S(1)} collective-permute-done((bf16[136,2176]{1,0:T(8,128)(2,1)S(1)}, bf16[136,2176]{1,0:T(8,128)(2,1)S(1)}, u32[]{:S(2)}, u32[]{:S(2)}) %collective-permute-start.6) | collective-permute-done | bytes 591904 | tf_op jit(solution)/shard_map/ppermute | solution.py:448
  160.1 19.0 %shard_map.135 = (bf16[512,1152]{1,0:T(8,128)(2,1)S(1)}, f32[17,512]{1,0:T(8,128)S(1)}) custom-call(bf16[512,3456]{1,0:T(8,128)(2,1)} %add_convert_fusion.own_ref, bf16[512,2304]{1,0:T(8,128)(2,1)S(1)} %collective-permute-done.4.other_ref, s32[1,512]{1,0:T(1,128)S(1)} %bitcast.130, s32[1024,1]{1,0:T(8,128)S(1)} %copy.65.key_ref), custom_call_target="tpu_custom_call" | custom-call | flops 21474836480 | bytes 12582912 | tf_op jit(solution)/shard_map/pallas_call | solution.py:422
  179.1 15.9 %collective-permute-done.8 = bf16[272,2176]{1,0:T(8,128)(2,1)S(1)} collective-permute-done((bf16[272,2176]{1,0:T(8,128)(2,1)S(1)}, bf16[272,2176]{1,0:T(8,128)(2,1)S(1)}, u32[]{:S(2)}, u32[]{:S(2)}) %collective-permute-start.8) | collective-permute-done | bytes 1183776 | tf_op jit(solution)/shard_map/ppermute | solution.py:448
  201.8 7.6 %fusion.107 = (f32[512]{0:T(512)}, f32[512,1088]{1,0:T(8,128)S(1)}) fusion(f32[1088]{0:T(1024)} %get-tuple-element.252, bf16[1280,4544]{1,0:T(8,128)(2,1)} %all-gather.3.cloned.1.call-done.mat_ref, bf16[512,1152]{1,0:T(8,128)(2,1)} %copy-done.20, bf16[1152,1280]{1,0:T(8,128)(2,1)} %fusion.4, bf16[512,1088]{1,0:T(8,128)(2,1)S(1)} %pad_maximum_fusion.8.input_ref), kind=kOutput, calls=%fused_computation.269 | convolution fusion | flops 2938895872 | bytes 10430464 | tf_op jit(solution)/shard_map/dot_general | solution.py:78
  227.8 7.4 %add_convert_fusion.4 = (bf16[512,2176]{1,0:T(8,128)(2,1)}, bf16[512,2176]{1,0:T(8,128)(2,1)S(1)}) fusion(f32[2176]{0:T(1024)S(1)} %copy-done.82, bf16[512,1088]{0,1:T(8,128)(2,1)S(1)} %convolution_convert_fusion.13, bf16[1088,2176]{1,0:T(8,128)(2,1)S(1)} %constant_dynamic-update-slice_fusion.1), kind=kOutput, calls=%fused_computation.38 | convolution fusion | flops 2446589952 | bytes 10314240 | tf_op jit(solution)/shard_map/dot_general | solution.py:78
  235.3 6.9 %add_convert_fusion.3 = (bf16[512,2176]{1,0:T(8,128)(2,1)}, bf16[512,2176]{1,0:T(8,128)(2,1)S(1)}) fusion(f32[2176]{0:T(1024)S(1)} %copy-done.81, bf16[512,1088]{0,1:T(8,128)(2,1)S(1)} %convolution_convert_fusion.12, bf16[1088,2176]{1,0:T(8,128)(2,1)S(1)} %constant_dynamic-update-slice_fusion.4), kind=kOutput, calls=%fused_computation.37 | convolution fusion | flops 2446589952 | bytes 10314240 | tf_op jit(solution)/shard_map/dot_general | solution.py:78
  243.5 9.5 %shard_map.136 = (bf16[4352,512]{1,0:T(8,128)(2,1)S(1)}, bf16[4352,576]{1,0:T(8,128)(2,1)S(1)}) custom-call(bf16[512,4352]{1,0:T(8,128)(2,1)S(1)} %pad_maximum_fusion.left_ref, bf16[512,1088]{1,0:T(8,128)(2,1)S(1)} %copy-done.7), custom_call_target="tpu_custom_call" | custom-call | flops 4848615424 | bytes 16777216 | tf_op jit(solution)/shard_map/pallas_call | solution.py:287
  259.1 7.0 %convert_reduce_fusion.1 = (bf16[2176]{0:T(1024)(128)(2,1)}, bf16[512,2176]{1,0:T(8,128)(2,1)S(1)}) fusion(bf16[512,2176]{1,0:T(8,128)(2,1)} %get-tuple-element.114, bf16[512,1088]{1,0:T(8,128)(2,1)S(1)} %copy-done.7, bf16[4352,1088]{1,0:T(8,128)(2,1)} %all-gather.5.cloned.1.call-done.mat_ref), kind=kOutput, calls=%fused_computation.35 | convolution fusion | flops 2429876224 | bytes 10588416 | tf_op jit(solution)/shard_map/dot_general | solution.py:39
  267.6 6.6 %convert_reduce_fusion.2 = (bf16[2176]{0:T(1024)(128)(2,1)}, bf16[512,2176]{1,0:T(8,128)(2,1)S(1)}) fusion(bf16[512,2176]{1,0:T(8,128)(2,1)} %get-tuple-element.113, bf16[512,1088]{1,0:T(8,128)(2,1)S(1)} %copy-done.7, bf16[4352,1088]{1,0:T(8,128)(2,1)S(1)} %copy-done.17), kind=kOutput, calls=%fused_computation.36 | convolution fusion | flops 2429876224 | bytes 10653952 | tf_op jit(solution)/shard_map/dot_general | solution.py:39
  290.2 6.2 %fusion.109 = bf16[512,1088]{0,1:T(8,128)(2,1)} fusion(bf16[512,2176]{1,0:T(8,128)(2,1)S(1)} %copy-done.94, bf16[1088,2176]{1,0:T(8,128)(2,1)} %copy-done.75), kind=kOutput, calls=%fused_computation.271 | convolution fusion | flops 2424307712 | bytes 8077312 | tf_op jit(solution)/shard_map/dot_general | solution.py:39
  322.7 6.8 %convolution_convert_fusion.10.grad_ref = bf16[512,1152]{1,0:T(8,128)(2,1)S(1)} fusion(bf16[1152,1280]{1,0:T(8,128)(2,1)} %fusion.4, bf16[512,1088]{1,0:T(8,128)(2,1)} %copy-done.68, bf16[1280,4544]{1,0:T(8,128)(2,1)} %all-gather.3.cloned.1.call-done.mat_ref), kind=kOutput, calls=%fused_computation.60 | convolution fusion | flops 2937257984 | bytes 8257536 | tf_op jit(solution)/shard_map/dot_general | solution.py:39
  335.3 11.6 %collective-permute-done.17 = bf16[4,2,136,512]{3,2,1,0:T(8,128)(2,1)} collective-permute-done((bf16[4,2,136,512]{3,2,1,0:T(8,128)(2,1)}, bf16[4,2,136,512]{3,2,1,0:T(8,128)(2,1)}, u32[]{:S(2)}, u32[]{:S(2)}) %collective-permute-start.17) | collective-permute-done | bytes 1114144 | tf_op jit(solution)/shard_map/ppermute | solution.py:448
  346.9 8.6 %collective-permute-done.18 = bf16[8,1,136,576]{3,2,0,1:T(8,128)(2,1)S(1)} collective-permute-done((bf16[8,1,136,576]{3,2,0,1:T(8,128)(2,1)}, bf16[8,1,136,576]{3,2,0,1:T(8,128)(2,1)S(1)}, u32[]{:S(2)}, u32[]{:S(2)}) %collective-permute-start.18) | collective-permute-done | bytes 1253408 | tf_op jit(solution)/shard_map/ppermute | solution.py:448
  366.0 26.7 %shard_map.137 = (bf16[512,3456]{1,0:T(8,128)(2,1)}, bf16[512,2304]{1,0:T(8,128)(2,1)S(1)}) custom-call(bf16[512,3456]{1,0:T(8,128)(2,1)} %add_convert_fusion.own_ref, bf16[512,2304]{1,0:T(8,128)(2,1)} %copy-done.19, s32[1,512]{1,0:T(1,128)S(1)} %bitcast.131, s32[1024,1]{1,0:T(8,128)S(1)} %copy-done.14, bf16[512,1152]{1,0:T(8,128)(2,1)S(1)} %copy-done.23, ...), custom_call_target="tpu_custom_call" | custom-call | flops 32212254720 | bytes 12582912 | tf_op jit(solution)/shard_map/pallas_call | solution.py:431
  392.7 15.5 %collective-permute-done.20 = bf16[272,2688]{1,0:T(8,128)(2,1)} collective-permute-done((bf16[272,2688]{1,0:T(8,128)(2,1)}, bf16[272,2688]{1,0:T(8,128)(2,1)}, u32[]{:S(2)}, u32[]{:S(2)}) %collective-permute-start.20) | collective-permute-done | bytes 1462304 | tf_op jit(solution)/shard_map/ppermute | solution.py:448
  417.6 13.2 %shard_map.138 = bf16[512,1088]{1,0:T(8,128)(2,1)S(1)} custom-call(bf16[512,4352]{1,0:T(8,128)(2,1)S(1)} %bitcast.125, bf16[4352,1088]{1,0:T(8,128)(2,1)S(1)} %copy-done.18, f32[512,1088]{1,0:T(8,128)S(1)} %copy-done.5, f32[1,1088]{1,0:T(1,128)S(1)} %broadcast_in_dim.24.bias_ref), custom_call_target="tpu_custom_call" | custom-call | flops 15032385536 | bytes 20971520 | tf_op jit(solution)/shard_map/pallas_call | solution.py:398
  444.8 6.2 %concatenate.128 = bf16[10880]{0:T(1024)(128)(2,1)} concatenate(bf16[1088]{0:T(1024)(128)(2,1)} %get-tuple-element.263, bf16[1088]{0:T(1024)(128)(2,1)} %get-tuple-element.262, bf16[1088]{0:T(1024)(128)(2,1)} %get-tuple-element.203, bf16[1088]{0:T(1024)(128)(2,1)} %get-tuple-element.199, bf16[1088]{0:T(1024)(128)(2,1)} %get-tuple-element.202, ...), dimensions={0} | concatenate | bytes 43520 | tf_op jit(solution)/shard_map/concatenate | solution.py:809
  470.3 16.2 %shard_map.140 = (bf16[512,1088]{1,0:T(8,128)(2,1)S(1)}, f32[1,1088]{1,0:T(1,128)S(1)}, f32[1,1088]{1,0:T(1,128)S(1)}) custom-call(bf16[512,3456]{1,0:T(8,128)(2,1)} %copy-done.1, bf16[1280,4544]{1,0:T(8,128)(2,1)} %all-gather.3.cloned.1.call-done.mat_ref, bf16[1088,1280]{1,0:T(8,128)(2,1)} %fusion.6.spread_ref, bf16[512,1088]{1,0:T(8,128)(2,1)S(1)} %copy-done.3, ...), custom_call_target="tpu_custom_call" | custom-call | flops 15032385536 | bytes 20971520 | tf_op jit(solution)/shard_map/pallas_call | solution.py:350
  505.2 8.4 %collective-permute-done.35 = bf16[34,5440]{1,0:T(8,128)(2,1)} collective-permute-done((bf16[34,5440]{1,0:T(8,128)(2,1)}, bf16[34,5440]{1,0:T(8,128)(2,1)}, u32[]{:S(2)}, u32[]{:S(2)}) %collective-permute-start.35) | collective-permute-done | bytes 369952 | tf_op jit(solution)/shard_map/ppermute | solution.py:448
  527.7 6.1 %collective-permute-done.36 = bf16[68,3456]{1,0:T(8,128)(2,1)} collective-permute-done((bf16[68,3456]{1,0:T(8,128)(2,1)}, bf16[68,3456]{1,0:T(8,128)(2,1)}, u32[]{:S(2)}, u32[]{:S(2)}) %collective-permute-start.36) | collective-permute-done | bytes 470048 | tf_op jit(solution)/shard_map/ppermute | solution.py:448
  551.9 9.2 %collective-permute-done.39 = bf16[34,3456]{1,0:T(8,128)(2,1)S(1)} collective-permute-done((bf16[34,3456]{1,0:T(8,128)(2,1)S(1)}, bf16[34,3456]{1,0:T(8,128)(2,1)S(1)}, u32[]{:S(2)}, u32[]{:S(2)}) %collective-permute-start.39) | collective-permute-done | bytes 235040 | tf_op jit(solution)/shard_map/ppermute | solution.py:448
  (495 shorter events, 248.3 us)
Async XLA Ops:
  7.2 110.6 %all-gather.3.cloned.1.call-start = ((), (), s32[]{:S(2)}) async-start(), calls=%async_computation.1 | async-start | bytes 12165120 | tf_op jit(solution)/shard_map/all_gather | solution.py:601
  11.3 247.7 %all-gather.5.cloned.1.call-start = ((), (), s32[]{:S(2)}) async-start(), calls=%async_computation.2 | async-start | bytes 10340352 | tf_op jit(solution)/shard_map/all_gather | solution.py:602
  11.8 29.0 %collective-permute-start = (bf16[34,4352]{1,0:T(8,128)(2,1)S(1)}, bf16[34,4352]{1,0:T(8,128)(2,1)S(1)}, u32[]{:S(2)}, u32[]{:S(2)}) collective-permute-start(bf16[34,4352]{1,0:T(8,128)(2,1)S(1)} %reshape.282), channel_id=1, source_target_pairs={{0,16},{4,20},{8,24},{12,28},{16,0},{20,4},{24,8},{28,12},{1,17},{... | collective-permute-start | bytes 887816 | tf_op jit(solution)/shard_map/ppermute | solution.py:448
  16.7 26.6 %collective-permute-start.3 = (bf16[256,1088]{0,1:T(8,128)(2,1)}, bf16[256,1088]{0,1:T(8,128)(2,1)}, u32[]{:S(2)}, u32[]{:S(2)}) collective-permute-start(bf16[256,1088]{0,1:T(8,128)(2,1)} %dynamic-slice_bitcast_fusion.5), channel_id=1, source_target_pairs={{0,2},{2,0},{1,3},{3,1},{4,6},{6,4},{5,7},{7,5},{8,10},{10,8},{9,1... | collective-permute-start | bytes 1671176 | tf_op jit(solution)/shard_map/ppermute | solution.py:545
  19.1 26.6 %collective-permute-start.2 = (bf16[256,1088]{0,1:T(8,128)(2,1)}, bf16[256,1088]{0,1:T(8,128)(2,1)}, u32[]{:S(2)}, u32[]{:S(2)}) collective-permute-start(bf16[256,1088]{0,1:T(8,128)(2,1)} %dynamic-slice_bitcast_fusion.6), channel_id=1, source_target_pairs={{0,2},{2,0},{1,3},{3,1},{4,6},{6,4},{5,7},{7,5},{8,10},{10,8},{9,1... | collective-permute-start | bytes 1671176 | tf_op jit(solution)/shard_map/ppermute | solution.py:545
  41.7 31.1 %collective-permute-start.1 = (bf16[68,4352]{1,0:T(8,128)(2,1)}, bf16[68,4352]{1,0:T(8,128)(2,1)}, u32[]{:S(2)}, u32[]{:S(2)}) collective-permute-start(bf16[68,4352]{1,0:T(8,128)(2,1)} %pad_maximum_fusion.13), channel_id=1, source_target_pairs={{0,8},{4,12},{8,0},{12,4},{16,24},{20,28},{24,16},{28,20},{1,9},{5... | collective-permute-start | bytes 1775624 | tf_op jit(solution)/shard_map/ppermute | solution.py:448
  136.0 24.0 %collective-permute-start.4 = (bf16[512,2304]{1,0:T(8,128)(2,1)S(1)}, bf16[512,2304]{1,0:T(8,128)(2,1)S(1)}, u32[]{:S(2)}, u32[]{:S(2)}) collective-permute-start(bf16[512,2304]{1,0:T(8,128)(2,1)S(1)} %slice.456), channel_id=1, source_target_pairs={{0,1},{1,0},{2,3},{3,2},{4,5},{5,4},{6,7},{7,6},{8,9},{9,8},{10,11... | collective-permute-start | bytes 7077896 | tf_op jit(solution)/shard_map/ppermute | solution.py:674
  157.7 37.4 %collective-permute-start.8 = (bf16[272,2176]{1,0:T(8,128)(2,1)S(1)}, bf16[272,2176]{1,0:T(8,128)(2,1)S(1)}, u32[]{:S(2)}, u32[]{:S(2)}) collective-permute-start(bf16[272,2176]{1,0:T(8,128)(2,1)S(1)} %pad_maximum_fusion.7), channel_id=1, source_target_pairs={{0,2},{2,0},{1,3},{3,1},{4,6},{6,4},{5,7},{7,5},{8,10},{10,8},{9,1... | collective-permute-start | bytes 3551240 | tf_op jit(solution)/shard_map/ppermute | solution.py:448
  158.5 39.4 %collective-permute-start.7 = (bf16[272,2176]{1,0:T(8,128)(2,1)S(1)}, bf16[272,2176]{1,0:T(8,128)(2,1)S(1)}, u32[]{:S(2)}, u32[]{:S(2)}) collective-permute-start(bf16[272,2176]{1,0:T(8,128)(2,1)S(1)} %pad_maximum_fusion.6), channel_id=1, source_target_pairs={{0,4},{4,0},{8,12},{12,8},{16,20},{20,16},{24,28},{28,24},{1,5},{5... | collective-permute-start | bytes 3551240 | tf_op jit(solution)/shard_map/ppermute | solution.py:448
  199.7 21.9 %collective-permute-start.10 = (bf16[544,2176]{1,0:T(8,128)(2,1)}, bf16[544,2176]{1,0:T(8,128)(2,1)}, u32[]{:S(2)}, u32[]{:S(2)}) collective-permute-start(bf16[544,2176]{1,0:T(8,128)(2,1)} %pad_maximum_fusion.4), channel_id=1, source_target_pairs={{0,1},{1,0},{2,3},{3,2},{4,5},{5,4},{6,7},{7,6},{8,9},{9,8},{10,11... | collective-permute-start | bytes 7102472 | tf_op jit(solution)/shard_map/ppermute | solution.py:448
  201.4 22.7 %collective-permute-start.9 = (bf16[544,2176]{1,0:T(8,128)(2,1)}, bf16[544,2176]{1,0:T(8,128)(2,1)}, u32[]{:S(2)}, u32[]{:S(2)}) collective-permute-start(bf16[544,2176]{1,0:T(8,128)(2,1)} %pad_maximum_fusion.3), channel_id=1, source_target_pairs={{0,1},{1,0},{2,3},{3,2},{4,5},{5,4},{6,7},{7,6},{8,9},{9,8},{10,11... | collective-permute-start | bytes 7102472 | tf_op jit(solution)/shard_map/ppermute | solution.py:448
  259.0 37.3 %collective-permute-start.13 = (bf16[16,1,136,512]{3,2,0,1:T(8,128)(2,1)}, bf16[16,1,136,512]{3,2,0,1:T(8,128)(2,1)}, u32[]{:S(2)}, u32[]{:S(2)}) collective-permute-start(bf16[16,1,136,512]{3,2,0,1:T(8,128)(2,1)} %dynamic-slice_bitcast_fusion.1), channel_id=1, source_target_pairs={{0,1},{1,0},{2,3},{3,2},{4,5},{5,4},{6,7},{7,6},{8,9},{9,8},{10,11... | collective-permute-start | bytes 6684680 | tf_op jit(solution)/shard_map/ppermute | solution.py:448
  318.7 28.2 %collective-permute-start.17 = (bf16[4,2,136,512]{3,2,1,0:T(8,128)(2,1)}, bf16[4,2,136,512]{3,2,1,0:T(8,128)(2,1)}, u32[]{:S(2)}, u32[]{:S(2)}) collective-permute-start(bf16[4,2,136,512]{3,2,1,0:T(8,128)(2,1)} %dynamic-slice_bitcast_fusion.3), channel_id=1, source_target_pairs={{0,4},{4,0},{8,12},{12,8},{16,20},{20,16},{24,28},{28,24},{1,5},{5... | collective-permute-start | bytes 3342344 | tf_op jit(solution)/shard_map/ppermute | solution.py:448
  322.7 32.8 %collective-permute-start.18 = (bf16[8,1,136,576]{3,2,0,1:T(8,128)(2,1)}, bf16[8,1,136,576]{3,2,0,1:T(8,128)(2,1)S(1)}, u32[]{:S(2)}, u32[]{:S(2)}) collective-permute-start(bf16[8,1,136,576]{3,2,0,1:T(8,128)(2,1)} %dynamic-slice_bitcast_fusion.2), channel_id=1, source_target_pairs={{0,2},{2,0},{1,3},{3,1},{4,6},{6,4},{5,7},{7,5},{8,10},{10,8},{9,1... | collective-permute-start | bytes 3760136 | tf_op jit(solution)/shard_map/ppermute | solution.py:448
  358.0 34.7 %collective-permute-start.22 = (bf16[4,1,136,512]{3,2,1,0:T(8,128)(2,1)}, bf16[4,1,136,512]{3,2,1,0:T(8,128)(2,1)}, u32[]{:S(2)}, u32[]{:S(2)}) collective-permute-start(bf16[4,1,136,512]{3,2,1,0:T(8,128)(2,1)} %constant_dynamic-slice_fusion.3), channel_id=1, source_target_pairs={{0,2},{2,0},{1,3},{3,1},{4,6},{6,4},{5,7},{7,5},{8,10},{10,8},{9,1... | collective-permute-start | bytes 1671176 | tf_op jit(solution)/shard_map/ppermute | solution.py:448
  359.6 33.1 %collective-permute-start.23 = (bf16[4,1,136,576]{3,2,0,1:T(8,128)(2,1)}, bf16[4,1,136,576]{3,2,0,1:T(8,128)(2,1)}, u32[]{:S(2)}, u32[]{:S(2)}) collective-permute-start(bf16[4,1,136,576]{3,2,0,1:T(8,128)(2,1)} %dynamic-slice_bitcast_fusion.4), channel_id=1, source_target_pairs={{0,4},{4,0},{8,12},{12,8},{16,20},{20,16},{24,28},{28,24},{1,5},{5... | collective-permute-start | bytes 1880072 | tf_op jit(solution)/shard_map/ppermute | solution.py:448
  361.3 46.9 %collective-permute-start.20 = (bf16[272,2688]{1,0:T(8,128)(2,1)}, bf16[272,2688]{1,0:T(8,128)(2,1)}, u32[]{:S(2)}, u32[]{:S(2)}) collective-permute-start(bf16[272,2688]{1,0:T(8,128)(2,1)} %slice.393), channel_id=1, source_target_pairs={{0,4},{4,0},{8,12},{12,8},{16,20},{20,16},{24,28},{28,24},{1,5},{5... | collective-permute-start | bytes 4386824 | tf_op jit(solution)/shard_map/ppermute | solution.py:448
  364.2 44.0 %collective-permute-start.21 = (bf16[272,2752]{1,0:T(8,128)(2,1)}, bf16[272,2752]{1,0:T(8,128)(2,1)S(1)}, u32[]{:S(2)}, u32[]{:S(2)}) collective-permute-start(bf16[272,2752]{1,0:T(8,128)(2,1)} %slice.394), channel_id=1, source_target_pairs={{0,2},{2,0},{1,3},{3,1},{4,6},{6,4},{5,7},{7,5},{8,10},{10,8},{9,1... | collective-permute-start | bytes 4491272 | tf_op jit(solution)/shard_map/ppermute | solution.py:448
  392.6 38.2 %collective-permute-start.19 = (bf16[512,2304]{1,0:T(8,128)(2,1)S(1)}, bf16[512,2304]{1,0:T(8,128)(2,1)S(1)}, u32[]{:S(2)}, u32[]{:S(2)}) collective-permute-start(bf16[512,2304]{1,0:T(8,128)(2,1)S(1)} %get-tuple-element.130), channel_id=1, source_target_pairs={{0,1},{1,0},{2,3},{3,2},{4,5},{5,4},{6,7},{7,6},{8,9},{9,8},{10,11... | collective-permute-start | bytes 7077896 | tf_op jit(solution)/shard_map/ppermute | solution.py:777
  465.7 20.9 %collective-permute-start.29 = (bf16[1,1,136,1088]{3,2,0,1:T(8,128)(2,1)S(1)}, bf16[1,1,136,1088]{3,2,0,1:T(8,128)(2,1)S(1)}, u32[]{:S(2)}, u32[]{:S(2)}) collective-permute-start(bf16[1,1,136,1088]{3,2,0,1:T(8,128)(2,1)S(1)} %constant_dynamic-slice_fusion.2), channel_id=1, source_target_pairs={{0,16},{4,20},{8,24},{12,28},{16,0},{20,4},{24,8},{28,12},{1,17},{... | collective-permute-start | bytes 887816 | tf_op jit(solution)/shard_map/ppermute | solution.py:448
  467.4 24.1 %collective-permute-start.32 = (bf16[68,5440]{1,0:T(8,128)(2,1)}, bf16[68,5440]{1,0:T(8,128)(2,1)S(1)}, u32[]{:S(2)}, u32[]{:S(2)}) collective-permute-start(bf16[68,5440]{1,0:T(8,128)(2,1)} %fusion.41), channel_id=1, source_target_pairs={{0,8},{4,12},{8,0},{12,4},{16,24},{20,28},{24,16},{28,20},{1,9},{5... | collective-permute-start | bytes 2219528 | tf_op jit(solution)/shard_map/ppermute | solution.py:448
  469.2 22.3 %collective-permute-start.30 = (bf16[272,1664]{1,0:T(8,128)(2,1)S(1)}, bf16[272,1664]{1,0:T(8,128)(2,1)S(1)}, u32[]{:S(2)}, u32[]{:S(2)}) collective-permute-start(bf16[272,1664]{1,0:T(8,128)(2,1)S(1)} %slice.409), channel_id=1, source_target_pairs={{0,4},{4,0},{8,12},{12,8},{16,20},{20,16},{24,28},{28,24},{1,5},{5... | collective-permute-start | bytes 2715656 | tf_op jit(solution)/shard_map/ppermute | solution.py:448
  470.0 21.5 %collective-permute-start.31 = (bf16[272,1792]{1,0:T(8,128)(2,1)S(1)}, bf16[272,1792]{1,0:T(8,128)(2,1)S(1)}, u32[]{:S(2)}, u32[]{:S(2)}) collective-permute-start(bf16[272,1792]{1,0:T(8,128)(2,1)S(1)} %slice.410), channel_id=1, source_target_pairs={{0,2},{2,0},{1,3},{3,1},{4,6},{6,4},{5,7},{7,5},{8,10},{10,8},{9,1... | collective-permute-start | bytes 2924552 | tf_op jit(solution)/shard_map/ppermute | solution.py:448
  503.8 20.8 %collective-permute-start.38 = (bf16[256,1088]{0,1:T(8,128)(2,1)}, bf16[256,1088]{0,1:T(8,128)(2,1)}, u32[]{:S(2)}, u32[]{:S(2)}) collective-permute-start(bf16[256,1088]{0,1:T(8,128)(2,1)} %copy.69), channel_id=1, source_target_pairs={{0,2},{2,0},{1,3},{3,1},{4,6},{6,4},{5,7},{7,5},{8,10},{10,8},{9,1... | collective-permute-start | bytes 1671176 | tf_op jit(solution)/shard_map/ppermute | solution.py:549
  (134 other events, 1777.0 us)
Sparse Core Ops, SparseCore 0:
  11.5 106.1 all-gather.2
  120.6 97.8 all-gather.4

commit v3 on v2

--- a/solution.py
+++ b/solution.py
@@ -604,10 +604,28 @@
         for step in order_a[:2:-1]:
             up_part = double(up_part, *step)
         up_cut = FF // 2
-        blocks, up_part, inputs, grad_rows, query_places, key_places, turn_a, turn_b, spread = tie(
+        up_a, up_b = up_part[:, :up_cut], up_part[:, up_cut:]
+        more_a, more_b = swap_with(up_a, *order_a[2]), swap_with(up_b, *order_b[2])
+        (
+            blocks,
+            up_a,
+            up_b,
+            more_a,
+            more_b,
+            inputs,
+            grad_rows,
+            query_places,
+            key_places,
+            turn_a,
+            turn_b,
+            spread,
+        ) = tie(
             (
                 blocks,
-                up_part,
+                up_a,
+                up_b,
+                more_a,
+                more_b,
                 inputs,
                 grad_rows,
                 query_places,
@@ -618,8 +636,9 @@
             )
         )
         head_a, head_b, head_spread = tie((head_a, head_b, head_spread))
-        up_a, up_b = up_part[:, :up_cut], up_part[:, up_cut:]
-        more_a, more_b = swap_with(up_a, *order_a[2]), swap_with(up_b, *order_b[2])
+        up_a = jnp.concatenate([up_a, more_a], axis=0)
+        up_b = jnp.concatenate([up_b, more_b], axis=0)
+        more_a, more_b = swap_with(up_a, *order_a[1]), swap_with(up_b, *order_b[1])
         grad_mat = blocks
         qkv_mat = blocks[:, : 3 * WIDE]
         out_mat = blocks[:, 3 * WIDE :]
@@ -674,16 +693,15 @@
     other = lax.ppermute(own[:, WIDE:], "core", SWAP)
     if whole_rows:
         one_a, one_b = turned(act_one, turn_a, turn_b)
-        one_a, one_b, more_a, more_b = tie((one_a, one_b, more_a, more_b))
+        other, one_a, one_b, more_a, more_b = tie((other, one_a, one_b, more_a, more_b))
         up_a = jnp.concatenate([up_a, more_a], axis=0)
         up_b = jnp.concatenate([up_b, more_b], axis=0)
-        more_a, more_b = swap_with(up_a, *order_a[1]), swap_with(up_b, *order_b[1])
-        other, one_a, one_b, up_a, up_b = tie((other, one_a, one_b, up_a, up_b))
+        more_a, more_b = swap_with(up_a, *order_a[0]), swap_with(up_b, *order_b[0])
     mixed, logs = attend(own, other, query_places, key_places)
     if whole_rows:
         mixed, more_a, more_b = tie((mixed, more_a, more_b))
-        up_a = double(jnp.concatenate([up_a, more_a], axis=0), *order_a[0])
-        up_b = double(jnp.concatenate([up_b, more_b], axis=0), *order_b[0])
+        up_a = jnp.concatenate([up_a, more_a], axis=0)
+        up_b = jnp.concatenate([up_b, more_b], axis=0)
         spread_mixed = round_low(dot_rows(mixed, head_spread))
     else:
         spread_mixed = mixed[:, :model_width]
@@ -760,31 +778,28 @@
         out_b = keep_first(mixed_b, grad_attn[:, out_cut:], out_got_b)
         rest_a = jnp.concatenate([sum_a, out_a], axis=1)
         rest_b = jnp.concatenate([sum_b, out_b], axis=1)
-        grad_mixed, rest_a, rest_b, down_got_a, down_got_b = tie(
-            (grad_mixed, rest_a, rest_b, down_got_a, down_got_b)
-        )
+        grad_mixed, rest_a, rest_b = tie((grad_mixed, rest_a, rest_b))
+        got_a, got_b = send_half(rest_a, *order_a[1]), send_half(rest_b, *order_b[1])
+    else:
+        sum_out = send_sum(mixed[:, :model_width], grad_attn)
+        grad_mixed = jnp.pad(grad_mixed, [(0, 0), (0, WIDE - model_width)])
+    early_small = jnp.concatenate(
+        [bias_out_term, gain_two_term, bias_two_term, up_bias_term, down_bias_term]
+    )
+    grad_own, grad_other = attend_back(
+        own, other, query_places, key_places, mixed, logs, grad_mixed
+    )
+    grad_got = lax.ppermute(grad_other, "core", SWAP)
+    if whole_rows:
+        grad_own, gelu_rows, early_small, got_a, got_b, down_got_a, down_got_b = tie(
+            (grad_own, gelu_rows, early_small, got_a, got_b, down_got_a, down_got_b)
+        )
+        rest_a, rest_b = add_half(rest_a, got_a), add_half(rest_b, got_b)
+        got_a, got_b = send_half(rest_a, *order_a[2]), send_half(rest_b, *order_b[2])
         down_a = add_block(down_a, down_got_a, *order_a[1], 2)
         down_b = add_block(down_b, down_got_b, *order_b[1], 1)
         down_got_a = send_block(down_a, *order_a[2], 1)
         down_got_b = send_block(down_b, *order_b[2], 1)
-        got_a, got_b = send_half(rest_a, *order_a[1]), send_half(rest_b, *order_b[1])
-    else:
-        sum_out = send_sum(mixed[:, :model_width], grad_attn)
-        grad_mixed = jnp.pad(grad_mixed, [(0, 0), (0, WIDE - model_width)])
-    grad_own, grad_other = attend_back(
-        own, other, query_places, key_places, mixed, logs, grad_mixed
-    )
-    grad_got = lax.ppermute(grad_other, "core", SWAP)
-    if whole_rows:
-        grad_own, got_a, got_b, gelu_rows, down_got_a, down_got_b = tie(
-            (grad_own, got_a, got_b, gelu_rows, down_got_a, down_got_b)
-        )
-        rest_a, rest_b = add_half(rest_a, got_a), add_half(rest_b, got_b)
-        got_a, got_b = send_half(rest_a, *order_a[2]), send_half(rest_b, *order_b[2])
-        down_a = add_block(down_a, down_got_a, *order_a[2], 1)
-        down_b = add_block(down_b, down_got_b, *order_b[2], 1)
-        sum_down = jnp.concatenate([down_a, down_b], axis=2)
-        down_got = send_block(sum_down, *order_a[3], 1)
     outputs = project(gelu_rows, down_mat, resid, down_bias[None, :])
     if whole_rows:
         grad_got, outputs = tie((grad_got, outputs))
@@ -797,26 +812,18 @@
         qkv_got_b = give_first(one_b, rows_b, order_b)
         qkv_a = keep_first(one_a, rows_a, qkv_got_a)
         qkv_b = keep_first(one_b, rows_b, qkv_got_b)
-        rows_now, qkv_a, qkv_b, got_a, got_b, down_got = tie(
-            (rows_now, qkv_a, qkv_b, got_a, got_b, down_got)
-        )
-        sum_down = add_block(sum_down, down_got, *order_a[3], 1)
+        rows_now, qkv_a, qkv_b, got_a, got_b, down_got_a, down_got_b = tie(
+            (rows_now, qkv_a, qkv_b, got_a, got_b, down_got_a, down_got_b)
+        )
+        down_a = add_block(down_a, down_got_a, *order_a[2], 1)
+        down_b = add_block(down_b, down_got_b, *order_b[2], 1)
+        sum_down = jnp.concatenate([down_a, down_b], axis=2)
+        down_got = send_block(sum_down, *order_a[3], 1)
         rest = jnp.concatenate([add_half(rest_a, got_a), add_half(rest_b, got_b)], axis=1)
         qkv_got_a = send_half(qkv_a, *order_a[1])
         qkv_got_b = send_half(qkv_b, *order_b[1])
         rest_got = send_half(rest, *order_a[3])
-    qkv_sums = jnp.sum(grad_qkv_rows.astype(jnp.float32), axis=0)
-    early_small = jnp.concatenate(
-        [
-            qkv_sums[:model_width],
-            qkv_sums[2 * WIDE : 2 * WIDE + model_width],
-            bias_out_term,
-            gain_two_term,
-            bias_two_term,
-            up_bias_term,
-            down_bias_term,
-        ]
-    )
+    qkv_sums = jnp.sum(rows_now.astype(jnp.float32), axis=0)
     grad_input, gain_one_term, bias_one_term = input_grad(
         rows_now, grad_mat, spread, low_inputs, gain_one[None, :], grad_resid
     )
@@ -825,19 +832,21 @@
             grad_input,
             gain_one_term,
             bias_one_term,
-            early_small,
+            qkv_sums,
             qkv_got_a,
             qkv_got_b,
             rest_got,
+            down_got,
         ) = tie(
             (
                 grad_input,
                 gain_one_term,
                 bias_one_term,
-                early_small,
+                qkv_sums,
                 qkv_got_a,
                 qkv_got_b,
                 rest_got,
+                down_got,
             )
         )
         qkv_a, qkv_b = add_half(qkv_a, qkv_got_a), add_half(qkv_b, qkv_got_b)
@@ -845,9 +854,18 @@
         qkv_got_b = send_half(qkv_b, *order_b[2])
         rest = add_half(rest, rest_got)
         rest_got = send_half(rest, *order_a[4])
+        sum_down = add_block(sum_down, down_got, *order_a[3], 1)
         for step in order_a[4:]:
             sum_down = add_block(sum_down, send_block(sum_down, *step, 1), *step, 1)
-    small_grad = jnp.concatenate([gain_one_term[0], bias_one_term[0], early_small])
+    small_grad = jnp.concatenate(
+        [
+            gain_one_term[0],
+            bias_one_term[0],
+            qkv_sums[:model_width],
+            qkv_sums[2 * WIDE : 2 * WIDE + model_width],
+            early_small,
+        ]
+    )
     small_grad = round_low(small_grad)
     if whole_rows:
         outputs, sum_down, qkv_got_a, qkv_got_b, rest_got = tie(

time: 580 us -> 598 us (1.031)
  local copies, waits for them, and re-layouts: 81.3 us -> 98.8 us
  waiting for transfers between devices: 173 us -> 165 us
    all_gather x1, waiting for transfers between devices: 43.6 us -> 22.9 us  [local(): blocks = lax.all_gather(blocks, ALL, axis=0, tiled=True)]
    unnamed x253 -> x235, local copies, waits for them, and re-layouts: 29.5 us -> 49.4 us
    ppermute x34, waiting for transfers between devices: 123 us -> 137 us  [swap_with(): lax.ppermute(values, axis, [(here, here ^ 1 << bit) for here in range(cou...]
  transfers between devices with their start and end apart: 43 -> 43, of which waited for: 18 -> 16; matrix products, arithmetic and copies ran while one was open for 35% -> 37% of each run, Pallas kernels for 15% -> 15%
where the time goes in v3:
time: 598 us; the launch traced here: 586 us
  waiting for transfers between devices  165 us (28%)
  matrix products  110 us (18%)
  local copies, waits for them, and re-layouts  98.8 us (17%)
  Pallas kernels  88.2 us (15%)
  other arithmetic  67.8 us (11%)
  starting transfers between devices  40.9 us (7%)
  between operations  15.9 us (3%)
    ppermute x34, waiting for transfers between devices, swap_with(): lax.ppermute(values, axis, [(here, here ^ 1 << bit) for here in range(cou...  137 us
    dot_general x10, matrix products, dot_rows(): lax.dot_general(left, right, (((1,), (0,)), ((), ())), preferred_element_...  53.1 us
    unnamed x235, local copies, waits for them, and re-layouts  49.4 us
    dot_general x7, matrix products, tail_dot(): lax.dot_general(left_side, right_side, (((1,), (1,)), ((), ())), preferre...  39.9 us
    ppermute x34, starting transfers between devices, swap_with(): lax.ppermute(values, axis, [(here, here ^ 1 << bit) for here in range(cou...  33.9 us
    pallas_call x1, Pallas kernels, attend_back(): return call(own, other, query_places, key_places, mixed, logs, grad)  27 us
    convert_element_type x21, other arithmetic, round_low(): return values.astype(jnp.bfloat16)  26.8 us
    all_gather x1, waiting for transfers between devices, local(): blocks = lax.all_gather(blocks, ALL, axis=0, tiled=True)  22.9 us
  transfers between devices with their start and end apart: 43, of which 16 were waited for; matrix products, arithmetic and copies ran while one was open for 37% of the time, Pallas kernels for 15%

profile of v3, /device:TPU:0, one launch (start us, length us, event | category | flops | bytes accessed | tf_op | source)
XLA Modules:
  0.0 586.5 jit_solution(3919087937644584279)
XLA Ops:
  45.7 27.3 %collective-permute-done.1 = bf16[68,4352]{1,0:T(8,128)(2,1)S(1)} collective-permute-done((bf16[68,4352]{1,0:T(8,128)(2,1)S(1)}, bf16[68,4352]{1,0:T(8,128)(2,1)S(1)}, u32[]{:S(2)}, u32[]{:S(2)}) %collective-permute-start.1) | collective-permute-done | bytes 591904 | tf_op jit(solution)/shard_map/ppermute | solution.py:448
  88.3 6.5 %collective-permute-done.3 = bf16[136,2176]{1,0:T(8,128)(2,1)} collective-permute-done((bf16[136,2176]{1,0:T(8,128)(2,1)S(1)}, bf16[136,2176]{1,0:T(8,128)(2,1)}, u32[]{:S(2)}, u32[]{:S(2)}) %collective-permute-start.3) | collective-permute-done | bytes 591904 | tf_op jit(solution)/shard_map/ppermute | solution.py:448
  97.7 22.9 %all-gather.3.cloned.1.call-done.mat_ref = bf16[1280,4544]{1,0:T(8,128)(2,1)} async-done(((bf16[40,4544]{1,0:T(8,128)(2,1)}), bf16[1280,4544]{1,0:T(8,128)(2,1)}) %all-gather.3.cloned.1.call-update) | async-done | bytes 11632656 | tf_op jit(solution)/shard_map/all_gather | solution.py:601
  127.5 13.0 %add_convert_fusion.own_ref = bf16[512,3456]{1,0:T(8,128)(2,1)} fusion(bf16[1280,4544]{1,0:T(8,128)(2,1)} %all-gather.3.cloned.1.call-done.mat_ref, f32[3456]{0:T(1024)S(1)} %reduce.2, bf16[1088,1280]{1,0:T(8,128)(2,1)} %fusion.6.spread_ref, bf16[512,1088]{1,0:T(8,128)(2,1)S(1)} %pad_maximum_fusion.8.input_ref, f32[1088]{0:T(1024)S(1)} %get-tuple-element.255, ...), kind=kOutput, calls=%fused_computation.3 | convolution fusion | flops 5963448320 | bytes 16312320 | tf_op jit(solution)/shard_map/dot_general | solution.py:78
  159.3 24.3 %collective-permute-done.7 = bf16[272,2176]{1,0:T(8,128)(2,1)} collective-permute-done((bf16[272,2176]{1,0:T(8,128)(2,1)}, bf16[272,2176]{1,0:T(8,128)(2,1)}, u32[]{:S(2)}, u32[]{:S(2)}) %collective-permute-start.7) | collective-permute-done | bytes 1183776 | tf_op jit(solution)/shard_map/ppermute | solution.py:448
  192.4 19.2 %shard_map.135 = (bf16[512,1152]{1,0:T(8,128)(2,1)S(1)}, f32[17,512]{1,0:T(8,128)S(1)}) custom-call(bf16[512,3456]{1,0:T(8,128)(2,1)} %add_convert_fusion.own_ref, bf16[512,2304]{1,0:T(8,128)(2,1)} %collective-permute-done.6.other_ref, s32[1,512]{1,0:T(1,128)S(1)} %bitcast.128, s32[1024,1]{1,0:T(8,128)S(1)} %copy.65.key_ref), custom_call_target="tpu_custom_call" | custom-call | flops 21474836480 | bytes 12582912 | tf_op jit(solution)/shard_map/pallas_call | solution.py:422
  214.8 7.6 %fusion.107 = (f32[512]{0:T(512)}, f32[512,1088]{1,0:T(8,128)S(1)}) fusion(f32[1088]{0:T(1024)S(1)} %copy-done.73, bf16[1280,4544]{1,0:T(8,128)(2,1)} %all-gather.3.cloned.1.call-done.mat_ref, bf16[512,1152]{1,0:T(8,128)(2,1)} %copy-done.16, bf16[1152,1280]{1,0:T(8,128)(2,1)} %fusion.4, bf16[512,1088]{1,0:T(8,128)(2,1)S(1)} %pad_maximum_fusion.8.input_ref), kind=kOutput, calls=%fused_computation.271 | convolution fusion | flops 2938895872 | bytes 10426624 | tf_op jit(solution)/shard_map/dot_general | solution.py:78
  232.9 10.0 %add_convert_fusion.4 = (bf16[512,2176]{1,0:T(8,128)(2,1)}, bf16[512,2176]{1,0:T(8,128)(2,1)S(1)}) fusion(f32[2176]{0:T(1024)S(1)} %copy-done.71, bf16[512,1088]{0,1:T(8,128)(2,1)S(1)} %convolution_convert_fusion.13, bf16[1088,2176]{1,0:T(8,128)(2,1)} %constant_dynamic-update-slice_fusion.1), kind=kOutput, calls=%fused_computation.38 | convolution fusion | flops 2446589952 | bytes 10314240 | tf_op jit(solution)/shard_map/dot_general | solution.py:78
  242.9 6.9 %add_convert_fusion.3 = (bf16[512,2176]{1,0:T(8,128)(2,1)}, bf16[512,2176]{1,0:T(8,128)(2,1)S(1)}) fusion(f32[2176]{0:T(1024)S(1)} %copy-done.70, bf16[512,1088]{0,1:T(8,128)(2,1)S(1)} %convolution_convert_fusion.12, bf16[1088,2176]{1,0:T(8,128)(2,1)S(1)} %bitcast.146), kind=kOutput, calls=%fused_computation.37 | convolution fusion | flops 2446589952 | bytes 10314240 | tf_op jit(solution)/shard_map/dot_general | solution.py:78
  251.1 9.7 %shard_map.136 = (bf16[4352,512]{1,0:T(8,128)(2,1)S(1)}, bf16[4352,576]{1,0:T(8,128)(2,1)S(1)}) custom-call(bf16[512,4352]{1,0:T(8,128)(2,1)S(1)} %pad_maximum_fusion.left_ref, bf16[512,1088]{1,0:T(8,128)(2,1)S(1)} %copy-done.4), custom_call_target="tpu_custom_call" | custom-call | flops 4848615424 | bytes 16777216 | tf_op jit(solution)/shard_map/pallas_call | solution.py:287
  270.3 7.4 %convert_reduce_fusion.1 = (bf16[2176]{0:T(1024)(128)(2,1)}, bf16[512,2176]{1,0:T(8,128)(2,1)S(1)}) fusion(bf16[512,2176]{1,0:T(8,128)(2,1)} %get-tuple-element.113, bf16[512,1088]{1,0:T(8,128)(2,1)} %pad_maximum_fusion.9.right_ref, bf16[4352,1088]{1,0:T(8,128)(2,1)} %all-gather.5.cloned.1.call-done.mat_ref), kind=kOutput, calls=%fused_computation.35 | convolution fusion | flops 2429876224 | bytes 10653952 | tf_op jit(solution)/shard_map/dot_general | solution.py:39
  279.9 6.5 %convert_reduce_fusion.2 = (bf16[2176]{0:T(1024)(128)(2,1)}, bf16[512,2176]{1,0:T(8,128)(2,1)S(1)}) fusion(bf16[512,2176]{1,0:T(8,128)(2,1)} %get-tuple-element.112, bf16[512,1088]{1,0:T(8,128)(2,1)S(1)} %copy-done.5, bf16[4352,1088]{1,0:T(8,128)(2,1)S(1)} %copy-done.14), kind=kOutput, calls=%fused_computation.36 | convolution fusion | flops 2429876224 | bytes 10653952 | tf_op jit(solution)/shard_map/dot_general | solution.py:39
  295.0 7.2 %fusion.108 = bf16[512,1088]{0,1:T(8,128)(2,1)} fusion(bf16[512,2176]{1,0:T(8,128)(2,1)} %copy-done.87, bf16[1088,2176]{1,0:T(8,128)(2,1)} %constant_dynamic-update-slice_fusion.1), kind=kOutput, calls=%fused_computation.272 | convolution fusion | flops 2424307712 | bytes 8077312 | tf_op jit(solution)/shard_map/dot_general | solution.py:39
  331.7 7.8 %convolution_convert_fusion.10.grad_ref = bf16[512,1152]{1,0:T(8,128)(2,1)} fusion(bf16[1152,1280]{1,0:T(8,128)(2,1)} %fusion.4, bf16[512,1088]{1,0:T(8,128)(2,1)} %copy-done.60, bf16[1280,4544]{1,0:T(8,128)(2,1)} %all-gather.3.cloned.1.call-done.mat_ref), kind=kOutput, calls=%fused_computation.60 | convolution fusion | flops 2937257984 | bytes 8257536 | tf_op jit(solution)/shard_map/dot_general | solution.py:39
  352.1 27.0 %shard_map.137 = (bf16[512,3456]{1,0:T(8,128)(2,1)}, bf16[512,2304]{1,0:T(8,128)(2,1)}) custom-call(bf16[512,3456]{1,0:T(8,128)(2,1)} %add_convert_fusion.own_ref, bf16[512,2304]{1,0:T(8,128)(2,1)} %collective-permute-done.6.other_ref, s32[1,512]{1,0:T(1,128)S(1)} %bitcast.129, s32[1024,1]{1,0:T(8,128)S(1)} %copy-done.13, bf16[512,1152]{1,0:T(8,128)(2,1)S(1)} %copy-done.19, ...), custom_call_target="tpu_custom_call" | custom-call | flops 32212254720 | bytes 12582912 | tf_op jit(solution)/shard_map/pallas_call | solution.py:431
  387.8 8.8 %collective-permute-done.19 = bf16[272,2752]{1,0:T(8,128)(2,1)} collective-permute-done((bf16[272,2752]{1,0:T(8,128)(2,1)}, bf16[272,2752]{1,0:T(8,128)(2,1)}, u32[]{:S(2)}, u32[]{:S(2)}) %collective-permute-start.19) | collective-permute-done | bytes 1497120 | tf_op jit(solution)/shard_map/ppermute | solution.py:448
  408.6 13.2 %shard_map.138 = bf16[512,1088]{1,0:T(8,128)(2,1)S(1)} custom-call(bf16[512,4352]{1,0:T(8,128)(2,1)S(1)} %copy-done.7, bf16[4352,1088]{1,0:T(8,128)(2,1)S(1)} %copy-done.15, f32[512,1088]{1,0:T(8,128)S(1)} %get-tuple-element.265.resid_ref, f32[1,1088]{1,0:T(1,128)S(1)} %broadcast_in_dim.24.bias_ref), custom_call_target="tpu_custom_call" | custom-call | flops 15032385536 | bytes 20971520 | tf_op jit(solution)/shard_map/pallas_call | solution.py:398
  436.7 12.1 %collective-permute-done.24 = bf16[136,2688]{1,0:T(8,128)(2,1)S(1)} collective-permute-done((bf16[136,2688]{1,0:T(8,128)(2,1)S(1)}, bf16[136,2688]{1,0:T(8,128)(2,1)S(1)}, u32[]{:S(2)}, u32[]{:S(2)}) %collective-permute-start.24) | collective-permute-done | bytes 731168 | tf_op jit(solution)/shard_map/ppermute | solution.py:448
  462.9 16.4 %shard_map.140 = (bf16[512,1088]{1,0:T(8,128)(2,1)S(1)}, f32[1,1088]{1,0:T(1,128)S(1)}, f32[1,1088]{1,0:T(1,128)S(1)}) custom-call(bf16[512,3456]{1,0:T(8,128)(2,1)} %copy-done.1, bf16[1280,4544]{1,0:T(8,128)(2,1)} %all-gather.3.cloned.1.call-done.mat_ref, bf16[1088,1280]{1,0:T(8,128)(2,1)} %fusion.6.spread_ref, ...), custom_call_target="tpu_custom_call" | custom-call | flops 15032385536 | bytes 20971520 | tf_op jit(solution)/shard_map/pallas_call | solution.py:350
  480.0 10.4 %collective-permute-done.30 = bf16[68,5440]{1,0:T(8,128)(2,1)S(1)} collective-permute-done((bf16[68,5440]{1,0:T(8,128)(2,1)}, bf16[68,5440]{1,0:T(8,128)(2,1)S(1)}, u32[]{:S(2)}, u32[]{:S(2)}) %collective-permute-start.30) | collective-permute-done | bytes 739872 | tf_op jit(solution)/shard_map/ppermute | solution.py:448
  507.6 15.2 %collective-permute-done.32 = bf16[1,1,136,1088]{3,2,0,1:T(8,128)(2,1)} collective-permute-done((bf16[1,1,136,1088]{3,2,0,1:T(8,128)(2,1)S(1)}, bf16[1,1,136,1088]{3,2,0,1:T(8,128)(2,1)}, u32[]{:S(2)}, u32[]{:S(2)}) %collective-permute-start.32) | collective-permute-done | bytes 295968 | tf_op jit(solution)/shard_map/ppermute | solution.py:448
  523.8 7.3 %collective-permute-done.35 = bf16[34,5440]{1,0:T(8,128)(2,1)} collective-permute-done((bf16[34,5440]{1,0:T(8,128)(2,1)}, bf16[34,5440]{1,0:T(8,128)(2,1)}, u32[]{:S(2)}, u32[]{:S(2)}) %collective-permute-start.35) | collective-permute-done | bytes 369952 | tf_op jit(solution)/shard_map/ppermute | solution.py:448
  545.4 6.1 %collective-permute-done.36 = bf16[68,3456]{1,0:T(8,128)(2,1)} collective-permute-done((bf16[68,3456]{1,0:T(8,128)(2,1)}, bf16[68,3456]{1,0:T(8,128)(2,1)}, u32[]{:S(2)}, u32[]{:S(2)}) %collective-permute-start.36) | collective-permute-done | bytes 470048 | tf_op jit(solution)/shard_map/ppermute | solution.py:448
  568.7 9.2 %collective-permute-done.39 = bf16[34,3456]{1,0:T(8,128)(2,1)S(1)} collective-permute-done((bf16[34,3456]{1,0:T(8,128)(2,1)S(1)}, bf16[34,3456]{1,0:T(8,128)(2,1)S(1)}, u32[]{:S(2)}, u32[]{:S(2)}) %collective-permute-start.39) | collective-permute-done | bytes 235040 | tf_op jit(solution)/shard_map/ppermute | solution.py:448
  (477 shorter events, 268.7 us)
Async XLA Ops:
  7.2 113.5 %all-gather.3.cloned.1.call-start = ((), (), s32[]{:S(2)}) async-start(), calls=%async_computation.1 | async-start | bytes 12165120 | tf_op jit(solution)/shard_map/all_gather | solution.py:601
  11.3 259.0 %all-gather.5.cloned.1.call-start = ((), (), s32[]{:S(2)}) async-start(), calls=%async_computation.2 | async-start | bytes 10340352 | tf_op jit(solution)/shard_map/all_gather | solution.py:602
  11.8 30.2 %collective-permute-start = (bf16[34,4352]{1,0:T(8,128)(2,1)S(1)}, bf16[34,4352]{1,0:T(8,128)(2,1)S(1)}, u32[]{:S(2)}, u32[]{:S(2)}) collective-permute-start(bf16[34,4352]{1,0:T(8,128)(2,1)S(1)} %reshape.282), channel_id=1, source_target_pairs={{0,16},{4,20},{8,24},{12,28},{16,0},{20,4},{24,8},{28,12},{1,17},{... | collective-permute-start | bytes 887816 | tf_op jit(solution)/shard_map/ppermute | solution.py:448
  16.7 27.1 %collective-permute-start.5 = (bf16[256,1088]{0,1:T(8,128)(2,1)}, bf16[256,1088]{0,1:T(8,128)(2,1)}, u32[]{:S(2)}, u32[]{:S(2)}) collective-permute-start(bf16[256,1088]{0,1:T(8,128)(2,1)} %dynamic-slice_bitcast_fusion.5), channel_id=1, source_target_pairs={{0,2},{2,0},{1,3},{3,1},{4,6},{6,4},{5,7},{7,5},{8,10},{10,8},{9,1... | collective-permute-start | bytes 1671176 | tf_op jit(solution)/shard_map/ppermute | solution.py:545
  19.1 57.4 %collective-permute-start.4 = (bf16[256,1088]{0,1:T(8,128)(2,1)}, bf16[256,1088]{0,1:T(8,128)(2,1)}, u32[]{:S(2)}, u32[]{:S(2)}) collective-permute-start(bf16[256,1088]{0,1:T(8,128)(2,1)} %dynamic-slice_bitcast_fusion.6), channel_id=1, source_target_pairs={{0,2},{2,0},{1,3},{3,1},{4,6},{6,4},{5,7},{7,5},{8,10},{10,8},{9,1... | collective-permute-start | bytes 1671176 | tf_op jit(solution)/shard_map/ppermute | solution.py:545
  42.1 30.9 %collective-permute-start.1 = (bf16[68,4352]{1,0:T(8,128)(2,1)S(1)}, bf16[68,4352]{1,0:T(8,128)(2,1)S(1)}, u32[]{:S(2)}, u32[]{:S(2)}) collective-permute-start(bf16[68,4352]{1,0:T(8,128)(2,1)S(1)} %pad_maximum_fusion.13), channel_id=1, source_target_pairs={{0,8},{4,12},{8,0},{12,4},{16,24},{20,28},{24,16},{28,20},{1,9},{5... | collective-permute-start | bytes 1775624 | tf_op jit(solution)/shard_map/ppermute | solution.py:448
  124.9 34.5 %collective-permute-start.8 = (bf16[272,2176]{1,0:T(8,128)(2,1)}, bf16[272,2176]{1,0:T(8,128)(2,1)}, u32[]{:S(2)}, u32[]{:S(2)}) collective-permute-start(bf16[272,2176]{1,0:T(8,128)(2,1)} %pad_maximum_fusion.7), channel_id=1, source_target_pairs={{0,2},{2,0},{1,3},{3,1},{4,6},{6,4},{5,7},{7,5},{8,10},{10,8},{9,1... | collective-permute-start | bytes 3551240 | tf_op jit(solution)/shard_map/ppermute | solution.py:448
  143.8 39.8 %collective-permute-start.6 = (bf16[512,2304]{1,0:T(8,128)(2,1)}, bf16[512,2304]{1,0:T(8,128)(2,1)}, u32[]{:S(2)}, u32[]{:S(2)}) collective-permute-start(bf16[512,2304]{1,0:T(8,128)(2,1)} %slice.460), channel_id=1, source_target_pairs={{0,1},{1,0},{2,3},{3,2},{4,5},{5,4},{6,7},{7,6},{8,9},{9,8},{10,11... | collective-permute-start | bytes 7077896 | tf_op jit(solution)/shard_map/ppermute | solution.py:693
  145.9 37.7 %collective-permute-start.7 = (bf16[272,2176]{1,0:T(8,128)(2,1)}, bf16[272,2176]{1,0:T(8,128)(2,1)}, u32[]{:S(2)}, u32[]{:S(2)}) collective-permute-start(bf16[272,2176]{1,0:T(8,128)(2,1)} %pad_maximum_fusion.6), channel_id=1, source_target_pairs={{0,4},{4,0},{8,12},{12,8},{16,20},{20,16},{24,28},{28,24},{1,5},{5... | collective-permute-start | bytes 3551240 | tf_op jit(solution)/shard_map/ppermute | solution.py:448
  267.0 40.7 %collective-permute-start.13 = (bf16[16,1,136,512]{3,2,0,1:T(8,128)(2,1)}, bf16[16,1,136,512]{3,2,0,1:T(8,128)(2,1)}, u32[]{:S(2)}, u32[]{:S(2)}) collective-permute-start(bf16[16,1,136,512]{3,2,0,1:T(8,128)(2,1)} %dynamic-slice_bitcast_fusion.1), channel_id=1, source_target_pairs={{0,1},{1,0},{2,3},{3,2},{4,5},{5,4},{6,7},{7,6},{8,9},{9,8},{10,11... | collective-permute-start | bytes 6684680 | tf_op jit(solution)/shard_map/ppermute | solution.py:448
  329.6 55.0 %collective-permute-start.20 = (bf16[4,2,136,512]{3,2,1,0:T(8,128)(2,1)}, bf16[4,2,136,512]{3,2,1,0:T(8,128)(2,1)}, u32[]{:S(2)}, u32[]{:S(2)}) collective-permute-start(bf16[4,2,136,512]{3,2,1,0:T(8,128)(2,1)} %dynamic-slice_bitcast_fusion.3), channel_id=1, source_target_pairs={{0,4},{4,0},{8,12},{12,8},{16,20},{20,16},{24,28},{28,24},{1,5},{5... | collective-permute-start | bytes 3342344 | tf_op jit(solution)/shard_map/ppermute | solution.py:448
  331.0 53.6 %collective-permute-start.21 = (bf16[8,1,136,576]{3,2,0,1:T(8,128)(2,1)}, bf16[8,1,136,576]{3,2,0,1:T(8,128)(2,1)}, u32[]{:S(2)}, u32[]{:S(2)}) collective-permute-start(bf16[8,1,136,576]{3,2,0,1:T(8,128)(2,1)} %dynamic-slice_bitcast_fusion.2), channel_id=1, source_target_pairs={{0,2},{2,0},{1,3},{3,1},{4,6},{6,4},{5,7},{7,5},{8,10},{10,8},{9,1... | collective-permute-start | bytes 3760136 | tf_op jit(solution)/shard_map/ppermute | solution.py:448
  347.6 40.2 %collective-permute-start.18 = (bf16[272,2688]{1,0:T(8,128)(2,1)}, bf16[272,2688]{1,0:T(8,128)(2,1)}, u32[]{:S(2)}, u32[]{:S(2)}) collective-permute-start(bf16[272,2688]{1,0:T(8,128)(2,1)} %slice.395), channel_id=1, source_target_pairs={{0,4},{4,0},{8,12},{12,8},{16,20},{20,16},{24,28},{28,24},{1,5},{5... | collective-permute-start | bytes 4386824 | tf_op jit(solution)/shard_map/ppermute | solution.py:448
  350.2 46.3 %collective-permute-start.19 = (bf16[272,2752]{1,0:T(8,128)(2,1)}, bf16[272,2752]{1,0:T(8,128)(2,1)}, u32[]{:S(2)}, u32[]{:S(2)}) collective-permute-start(bf16[272,2752]{1,0:T(8,128)(2,1)} %slice.396), channel_id=1, source_target_pairs={{0,2},{2,0},{1,3},{3,1},{4,6},{6,4},{5,7},{7,5},{8,10},{10,8},{9,1... | collective-permute-start | bytes 4491272 | tf_op jit(solution)/shard_map/ppermute | solution.py:448
  379.1 42.8 %collective-permute-start.17 = (bf16[512,2304]{1,0:T(8,128)(2,1)}, bf16[512,2304]{1,0:T(8,128)(2,1)}, u32[]{:S(2)}, u32[]{:S(2)}) collective-permute-start(bf16[512,2304]{1,0:T(8,128)(2,1)} %get-tuple-element.127), channel_id=1, source_target_pairs={{0,1},{1,0},{2,3},{3,2},{4,5},{5,4},{6,7},{7,6},{8,9},{9,8},{10,11... | collective-permute-start | bytes 7077896 | tf_op jit(solution)/shard_map/ppermute | solution.py:792
  398.5 38.2 %collective-permute-start.26 = (bf16[4,1,136,512]{3,2,1,0:T(8,128)(2,1)S(1)}, bf16[4,1,136,512]{3,2,1,0:T(8,128)(2,1)S(1)}, u32[]{:S(2)}, u32[]{:S(2)}) collective-permute-start(bf16[4,1,136,512]{3,2,1,0:T(8,128)(2,1)S(1)} %constant_dynamic-slice_fusion.3), channel_id=1, source_target_pairs={{0,2},{2,0},{1,3},{3,1},{4,6},{6,4},{5,7},{7,5},{8,10},{10,8},{9,1... | collective-permute-start | bytes 1671176 | tf_op jit(solution)/shard_map/ppermute | solution.py:448
  401.0 35.7 %collective-permute-start.27 = (bf16[4,1,136,576]{3,2,0,1:T(8,128)(2,1)S(1)}, bf16[4,1,136,576]{3,2,0,1:T(8,128)(2,1)S(1)}, u32[]{:S(2)}, u32[]{:S(2)}) collective-permute-start(bf16[4,1,136,576]{3,2,0,1:T(8,128)(2,1)S(1)} %dynamic-slice_bitcast_fusion.4), channel_id=1, source_target_pairs={{0,4},{4,0},{8,12},{12,8},{16,20},{20,16},{24,28},{28,24},{1,5},{5... | collective-permute-start | bytes 1880072 | tf_op jit(solution)/shard_map/ppermute | solution.py:448
  460.9 29.5 %collective-permute-start.30 = (bf16[68,5440]{1,0:T(8,128)(2,1)}, bf16[68,5440]{1,0:T(8,128)(2,1)S(1)}, u32[]{:S(2)}, u32[]{:S(2)}) collective-permute-start(bf16[68,5440]{1,0:T(8,128)(2,1)} %fusion.41), channel_id=1, source_target_pairs={{0,8},{4,12},{8,0},{12,4},{16,24},{20,28},{24,16},{28,20},{1,9},{5... | collective-permute-start | bytes 2219528 | tf_op jit(solution)/shard_map/ppermute | solution.py:448
  461.9 28.5 %collective-permute-start.28 = (bf16[272,1664]{1,0:T(8,128)(2,1)}, bf16[272,1664]{1,0:T(8,128)(2,1)}, u32[]{:S(2)}, u32[]{:S(2)}) collective-permute-start(bf16[272,1664]{1,0:T(8,128)(2,1)} %slice.408), channel_id=1, source_target_pairs={{0,4},{4,0},{8,12},{12,8},{16,20},{20,16},{24,28},{28,24},{1,5},{5... | collective-permute-start | bytes 2715656 | tf_op jit(solution)/shard_map/ppermute | solution.py:448
  462.2 28.1 %collective-permute-start.29 = (bf16[272,1792]{1,0:T(8,128)(2,1)S(1)}, bf16[272,1792]{1,0:T(8,128)(2,1)S(1)}, u32[]{:S(2)}, u32[]{:S(2)}) collective-permute-start(bf16[272,1792]{1,0:T(8,128)(2,1)S(1)} %slice.409), channel_id=1, source_target_pairs={{0,2},{2,0},{1,3},{3,1},{4,6},{6,4},{5,7},{7,5},{8,10},{10,8},{9,1... | collective-permute-start | bytes 2924552 | tf_op jit(solution)/shard_map/ppermute | solution.py:448
  501.3 29.8 %collective-permute-start.35 = (bf16[34,5440]{1,0:T(8,128)(2,1)}, bf16[34,5440]{1,0:T(8,128)(2,1)}, u32[]{:S(2)}, u32[]{:S(2)}) collective-permute-start(bf16[34,5440]{1,0:T(8,128)(2,1)} %slice.489), channel_id=1, source_target_pairs={{0,16},{4,20},{8,24},{12,28},{16,0},{20,4},{24,8},{28,12},{1,17},{... | collective-permute-start | bytes 1109768 | tf_op jit(solution)/shard_map/ppermute | solution.py:448
  502.4 28.7 %collective-permute-start.33 = (bf16[136,1664]{1,0:T(8,128)(2,1)}, bf16[136,1664]{1,0:T(8,128)(2,1)}, u32[]{:S(2)}, u32[]{:S(2)}) collective-permute-start(bf16[136,1664]{1,0:T(8,128)(2,1)} %slice.487), channel_id=1, source_target_pairs={{0,2},{2,0},{1,3},{3,1},{4,6},{6,4},{5,7},{7,5},{8,10},{10,8},{9,1... | collective-permute-start | bytes 1357832 | tf_op jit(solution)/shard_map/ppermute | solution.py:448
  503.5 27.6 %collective-permute-start.34 = (bf16[136,1792]{1,0:T(8,128)(2,1)}, bf16[136,1792]{1,0:T(8,128)(2,1)}, u32[]{:S(2)}, u32[]{:S(2)}) collective-permute-start(bf16[136,1792]{1,0:T(8,128)(2,1)} %slice.488), channel_id=1, source_target_pairs={{0,4},{4,0},{8,12},{12,8},{16,20},{20,16},{24,28},{28,24},{1,5},{5... | collective-permute-start | bytes 1462280 | tf_op jit(solution)/shard_map/ppermute | solution.py:448
  506.0 36.2 %collective-permute-start.38 = (bf16[256,1088]{0,1:T(8,128)(2,1)}, bf16[256,1088]{0,1:T(8,128)(2,1)}, u32[]{:S(2)}, u32[]{:S(2)}) collective-permute-start(bf16[256,1088]{0,1:T(8,128)(2,1)} %copy.69), channel_id=1, source_target_pairs={{0,2},{2,0},{1,3},{3,1},{4,6},{6,4},{5,7},{7,5},{8,10},{10,8},{9,1... | collective-permute-start | bytes 1671176 | tf_op jit(solution)/shard_map/ppermute | solution.py:549
  (124 other events, 1172.1 us)
Sparse Core Ops, SparseCore 0:
  11.5 109.0 all-gather.2
  123.5 98.2 all-gather.4
